TPU v7x, 32 devices: a whole 2x2x4 slice. The times are simulated.
32 devices in a mesh: row: 4 (over y, x), col: 8 (over z, core).
Axes of the slice: x: 2, y: 2, z: 4, core: 2. Of those that a mesh axis runs over, the one named last changes fastest.
Arguments:
- state: float32 [6, 137, 128, 512], P(None, None, 'col', 'row'), may hold values from -2 to 2, as said below
- conv_mask: int32 [128, 512], P('col', 'row'), may hold values from 0 to 1, as said below
- micro_mask: int32 [128, 512], P('col', 'row'), may hold values from 0 to 1, as said below
- w_in: bfloat16 [1024, 822], replicated, may hold values from -0.21875 to 0.21875
- w_hidden: bfloat16 [2, 1024, 1024], replicated, may hold values from -0.1875 to 0.1875
- w_out: bfloat16 [548, 1024], replicated, may hold values from -0.03125 to 0.03125
Outputs:
- advanced: float32 [6, 137, 128, 512], P(None, None, 'col', 'row')
- tendency: float32 [6, 137, 128, 512], P(None, None, 'col', 'row')
Inputs may be any that keep to these rules, and one draw needn't show every extreme that they name: `state`: temperature, vapour, cloud water and rain lie in 0.2 to 2, the two winds in -2 to 2. `conv_mask`: 1 marks an active column; activity is clustered in tiles of 16 x 128 columns. `micro_mask`: 1 marks an active column; activity is clustered in tiles of 16 x 128 columns.
All inputs are finite; a program needn't handle non-finite values.
Results may differ from a plain program's by a relative error of at most 0.00053.
Values sent between devices are 32-bit elements; how exact they have to be, the bound alone decides.
A program may use at most 192 MiB of HBM per device.

v0:
```python
import jax
import jax.numpy as jnp
from jax import lax
from jax.sharding import PartitionSpec as P

ITERS = 3


def padded(cells, sides, width, closed):
    for axis, dim in sides:
        count = lax.axis_size(axis)
        ends = count if closed else count - 1
        head = lax.slice_in_dim(cells, 0, width, axis=dim)
        tail = lax.slice_in_dim(cells, cells.shape[dim] - width, cells.shape[dim], axis=dim)
        cells = jnp.concatenate(
            [
                lax.ppermute(tail, axis, [(i, (i + 1) % count) for i in range(ends)]),
                cells,
                lax.ppermute(head, axis, [((i + 1) % count, i) for i in range(ends)]),
            ],
            axis=dim,
        )
    return cells


def column_tend(cols, conv, micro, w_in, w_hidden, w_out):
    fields, levels, count = cols.shape
    z = cols.reshape(fields * levels, count).astype(jnp.bfloat16)
    hidden = jax.nn.silu(jnp.dot(w_in, z, preferred_element_type=jnp.float32)).astype(jnp.bfloat16)
    hidden = jax.nn.silu(jnp.dot(w_hidden[0], hidden, preferred_element_type=jnp.float32)).astype(
        jnp.bfloat16
    )
    hidden = jax.nn.silu(jnp.dot(w_hidden[1], hidden, preferred_element_type=jnp.float32)).astype(
        jnp.bfloat16
    )
    network_out = jnp.dot(w_out, hidden, preferred_element_type=jnp.float32).reshape(
        4, levels, count
    )
    temp, vapour, water = (cols[0], cols[1], cols[2])
    for step in range(ITERS):
        satur = 0.5 * jnp.exp(0.5 * temp)
        delta = jnp.maximum(0.5 * (vapour - satur), -water)
        temp = temp + 0.5 * delta
        vapour = vapour - delta
        water = water + delta
    autoconv = 0.6 * jnp.maximum(water - 0.8, 0.0)
    water = water - autoconv
    return jnp.stack(
        [
            conv * network_out[0] + micro * (temp - cols[0]),
            conv * network_out[1] + micro * (vapour - cols[1]),
            micro * (water - cols[2]),
            micro * autoconv,
            conv * network_out[2],
            conv * network_out[3],
        ]
    )


def advance(ext):

    def shifted(a, b):
        return ext[..., 2 + a : ext.shape[-2] - 2 + a, 2 + b : ext.shape[-1] - 2 + b]

    center = shifted(0, 0)
    along_x = (8.0 * (shifted(1, 0) - shifted(-1, 0)) - (shifted(2, 0) - shifted(-2, 0))) / 12.0
    along_y = (8.0 * (shifted(0, 1) - shifted(0, -1)) - (shifted(0, 2) - shifted(0, -2))) / 12.0
    hyper = (
        shifted(2, 0)
        + shifted(-2, 0)
        + shifted(0, 2)
        + shifted(0, -2)
        - 4.0 * (shifted(1, 0) + shifted(-1, 0) + shifted(0, 1) + shifted(0, -1))
        + 12.0 * center
    )
    return center - 0.15 * (center[4] * along_x + center[5] * along_y) - 0.06 * hyper


def active_ranks(flags):
    valid = flags[0] + flags[1] > 0.0
    ranks = jnp.cumsum(valid.astype(jnp.int32)) - 1
    return (valid, ranks)


def physics_set(cols, flags, w_in, w_hidden, w_out):
    width = cols.shape[2]
    valid, ranks = active_ranks(flags)
    count = jnp.sum(valid.astype(jnp.int32))
    order = jnp.full((width,), width, jnp.int32)
    order = order.at[jnp.where(valid, ranks, width)].set(
        jnp.arange(width, dtype=jnp.int32), mode="drop"
    )
    packed = jnp.take(cols, order, axis=2, mode="clip")
    packed_flags = jnp.take(flags, order, axis=1, mode="fill", fill_value=0.0)
    blocks = (count + 127) // 128

    def one_block(index, total):
        start = index * 128
        block = lax.dynamic_slice_in_dim(packed, start, 128, 2)
        marks = lax.dynamic_slice_in_dim(packed_flags, start, 128, 1)
        result = column_tend(block, marks[0], marks[1], w_in, w_hidden, w_out)
        return lax.dynamic_update_slice_in_dim(total, result, start, 2)

    done = lax.fori_loop(0, blocks, one_block, jnp.zeros(cols.shape, jnp.float32))
    placed = jnp.take(done, jnp.maximum(ranks, 0), axis=2, mode="clip")
    return jnp.where(valid[None, None, :], placed, 0.0)


def local(state, conv_mask, micro_mask, w_in, w_hidden, w_out):
    fields, levels, lon_cells, lat_cells = state.shape
    width = lon_cells * lat_cells
    cols = state.reshape(fields, levels, width)
    flags = jnp.stack([conv_mask, micro_mask]).astype(jnp.float32).reshape(2, width)
    tend_cols = physics_set(cols, flags, w_in, w_hidden, w_out)
    tendency = tend_cols.reshape(fields, levels, lon_cells, lat_cells)
    current = state + tendency
    for step in range(2):
        ext = padded(current, (("col", 2),), 2, True)
        ext = padded(ext, (("row", 3),), 2, False)
        current = advance(ext)
    return (current, tendency)


def solution(mesh):
    in_specs = (P(None, None, "col", "row"), P("col", "row"), P("col", "row"), P(), P(), P())
    out_specs = (P(None, None, "col", "row"), P(None, None, "col", "row"))
    return jax.shard_map(local, mesh=mesh, in_specs=in_specs, out_specs=out_specs, check_vma=False)
```

profile of v0, /device:TPU:0, one launch (start us, length us, event | category | flops | bytes accessed | tf_op | source)
XLA Modules:
  0.0 535.6 jit_solution(12775211995938329054)
XLA Ops:
  3.3 8.0 %scatter_custom_fusion = s32[2048]{0:T(1024)S(1)} fusion(s32[2048]{0:T(1024)S(1)} %bitcast.139, s32[2048]{0:T(1024)S(1)} %iota.3, s32[]{:T(128)} %constant.100.clone.1), kind=kCustom, calls=%fused_computation.114 | custom fusion | bytes 8196 | tf_op jit(solution)/shard_map/scatter | solution.py:90
  12.5 5.5 %gather_fusion = f32[2048,2]{1,0:T(8,128)S(1)} fusion(f32[2,2048]{0,1:T(8,128)S(1)} %copy.16, s32[2048]{0:T(1024)S(1)} %get-tuple-element.175), kind=kCustom, calls=%fused_computation | custom fusion | bytes 40960 | tf_op jit(solution)/shard_map/jit(_take)/gather | solution.py:94
  18.6 11.8 %copy.17 = f32[6,137,16,128]{1,0,3,2:T(8,128)} copy(f32[6,137,16,128]{3,2,1,0:T(8,128)} %param.8) | data formatting | bytes 13467648 | tf_op args[0]
  30.5 24.6 %gather_fusion.1 = f32[2048,6,137]{2,1,0:T(8,128)} fusion(f32[6,137,2048]{1,0,2:T(8,128)} %bitcast.128, s32[2048]{0:T(1024)S(1)} %get-tuple-element.174), kind=kCustom, calls=%fused_computation.1 | custom fusion | bytes 13475840 | tf_op jit(solution)/shard_map/jit(_take)/gather | solution.py:93
  55.1 13.0 %copy.19 = f32[6,137,2048]{2,1,0:T(8,128)} copy(f32[6,137,2048]{1,0,2:T(8,128)} %bitcast.129) | data formatting | bytes 13467648 | tf_op jit(solution)/shard_map/while | solution.py:104
  68.1 3.8 broadcast_in_dim.37
  71.9 90.2 %while.12 = (s32[]{:T(128)}, f32[6,137,2048]{2,1,0:T(8,128)}, s32[]{:T(128)}, f32[2,2048]{1,0:T(2,128)S(1)}, f32[6,137,2048]{2,1,0:T(8,128)}, /*index=5*/bf16[10...) while((s32[]{:T(128)}, f32[6,137,2048]{2,1,0:T(8,128)}, ...), condition=%wide.region_5.6_spmd, body=%wide.region_4.5_spmd.sunk | while | flops 898886272 | bytes 11629299 | solution.py:104
  71.9 1.0 dynamic-slice_convert_fusion.2
  73.0 3.4 multiply_convert_fusion.4
  76.4 2.9 convolution_bitcast_fusion.3
  79.3 1.1 fusion.71
  83.2 1.0 dynamic-slice_convert_fusion.2
  84.3 3.4 multiply_convert_fusion.4
  87.6 2.9 convolution_bitcast_fusion.3
  90.6 1.1 fusion.71
  95.5 3.4 multiply_convert_fusion.4
  98.9 2.9 convolution_bitcast_fusion.3
  101.8 1.1 fusion.71
  106.8 3.4 multiply_convert_fusion.4
  110.2 2.9 convolution_bitcast_fusion.3
  113.1 1.1 fusion.71
  118.0 3.4 multiply_convert_fusion.4
  121.4 2.9 convolution_bitcast_fusion.3
  124.3 1.1 fusion.71
  128.2 1.0 dynamic-slice_convert_fusion.2
  129.3 3.4 multiply_convert_fusion.4
  132.7 2.9 convolution_bitcast_fusion.3
  135.6 1.1 fusion.71
  140.6 3.4 multiply_convert_fusion.4
  144.0 2.9 convolution_bitcast_fusion.3
  146.9 1.1 fusion.71
  151.9 3.4 multiply_convert_fusion.4
  155.3 2.9 convolution_bitcast_fusion.3
  158.2 1.1 fusion.71
  162.1 12.4 %copy.20 = f32[6,137,2048]{1,0,2:T(8,128)} copy(f32[6,137,2048]{2,1,0:T(8,128)} %get-tuple-element.106) | data formatting | bytes 13467648 | tf_op jit(solution)/shard_map/while | solution.py:104
  174.5 24.6 %gather_fusion.2 = f32[2048,6,137]{2,1,0:T(8,128)} fusion(f32[6,137,2048]{1,0,2:T(8,128)} %copy.20, s32[2048]{0:T(1024)S(1)} %broadcast_clamp_fusion), kind=kCustom, calls=%fused_computation.2 | custom fusion | bytes 13475840 | tf_op jit(solution)/shard_map/jit(_take)/gather | solution.py:105
  199.2 12.0 %copy.21 = f32[6,137,16,128]{3,1,2,0:T(8,128)} copy(f32[6,137,16,128]{1,0,3,2:T(8,128)} %bitcast.130) | data formatting | bytes 13467648 | tf_op jit(solution)/shard_map/jit(_take)/gather | solution.py:105
  211.2 12.5 %copy_add_fusion = (f32[6,137,16,128]{3,1,2,0:T(8,128)}, f32[6,137,16,128]{3,1,2,0:T(8,128)}) fusion(f32[6,137,16,128]{3,2,1,0:T(8,128)} %param.8, f32[6,137,16,128]{3,1,2,0:T(8,128)} %copy.21, pred[16,128]{1,0:T(8,128)(4,1)S(1)} %bitcast.132), kind=kLoop, calls=%fused_computation.86 | loop fusion | flops 3366912 | bytes 26937344 | tf_op jit(solution)/shard_map/add | solution.py:116
  223.7 1.5 fusion.50
  225.8 16.8 %collective-permute-done = f32[6,137,2,128]{3,1,2,0:T(8,128)S(1)} collective-permute-done((f32[6,137,2,128]{3,1,2,0:T(8,128)S(1)}, f32[6,137,2,128]{3,1,2,0:T(8,128)S(1)}, u32[]{:S(2)}, u32[]{:S(2)}) %collective-permute-start) | collective-permute-done | bytes 841760 | tf_op jit(solution)/shard_map/ppermute | solution.py:19
  243.5 3.4 pad_maximum_fusion
  246.9 7.5 %fusion.48 = (f32[6,137,20,2]{3,1,2,0:T(8,128)}, f32[6,137,20,2]{3,1,2,0:T(8,128)}) fusion(f32[6,137,20,128]{3,1,2,0:T(8,128)S(1)} %pad_maximum_fusion), kind=kLoop, calls=%fused_computation.118 | loop fusion | bytes 526080 | tf_op jit(solution)/shard_map/slice | solution.py:14
  254.4 7.2 %copy.23 = f32[6,137,20,2]{1,2,3,0:T(8,128)S(1)} copy(f32[6,137,20,2]{3,1,2,0:T(8,128)} %get-tuple-element.163) | data formatting | bytes 263040 | tf_op jit(solution)/shard_map/slice | solution.py:13
  261.7 1.3 collective-permute-start.2
  263.0 7.9 %copy.25 = f32[6,137,20,2]{1,2,3,0:T(8,128)} copy(f32[6,137,20,2]{3,1,2,0:T(8,128)} %get-tuple-element.162) | data formatting | bytes 263040 | tf_op jit(solution)/shard_map/slice | solution.py:14
  270.9 103.2 %collective-permute-start.3 = (f32[6,137,20,2]{1,2,3,0:T(8,128)}, f32[6,137,20,2]{1,2,3,0:T(8,128)}, u32[]{:S(2)}, u32[]{:S(2)}) collective-permute-start(f32[6,137,20,2]{1,2,3,0:T(8,128)} %copy.25), channel_id=1, source_target_pairs={{0,8},{8,16},{16,24},{1,9},{9,17},{17,25},{2,10},{10,18},{18,26},{... | collective-permute-start | bytes 394568 | tf_op jit(solution)/shard_map/ppermute | solution.py:17
  374.0 1.8 fusion.40
  375.9 6.1 %copy.24 = f32[6,137,20,2]{3,1,2,0:T(8,128)} copy(f32[6,137,20,2]{1,2,3,0:T(8,128)} %collective-permute-done.2) | data formatting | bytes 263040 | tf_op jit(solution)/shard_map/ppermute | solution.py:19
  382.0 6.0 %copy.26 = f32[6,137,20,2]{3,1,2,0:T(8,128)} copy(f32[6,137,20,2]{1,2,3,0:T(8,128)} %collective-permute-done.3) | data formatting | bytes 263040 | tf_op jit(solution)/shard_map/ppermute | solution.py:17
  387.9 36.1 %multiply_subtract_fusion.1 = f32[6,137,16,128]{3,1,2,0:T(8,128)} fusion(f32[6,137,16,128]{3,1,2,0:T(8,128)} %get-tuple-element.154, f32[6,137,20,2]{3,1,2,0:T(8,128)} %copy.24, f32[6,137,2,128]{3,1,2,0:T(8,128)S(1)} %collective-permute-done, f32[6,137,2,128]{3,1,2,0:T(8,128)} %copy-done.1, f32[6,137,20,2]{3,1,2,0:T(8,128)} %copy.26, ...), kind=kLoop, calls=%fused_computation.88 | loop fusion | flops 69021696 | bytes 17658752 | tf_op jit(solution)/shard_map/sub | solution.py:76
  424.0 1.6 fusion.49
  426.4 8.3 %copy.32 = f32[6,137,16,128]{3,2,1,0:T(8,128)} copy(f32[6,137,16,128]{3,1,2,0:T(8,128)} %get-tuple-element.155) | data formatting | bytes 13467648
  434.7 10.8 %collective-permute-done.4 = f32[6,137,2,128]{3,1,2,0:T(8,128)S(1)} collective-permute-done((f32[6,137,2,128]{3,1,2,0:T(8,128)S(1)}, f32[6,137,2,128]{3,1,2,0:T(8,128)S(1)}, u32[]{:S(2)}, u32[]{:S(2)}) %collective-permute-start.4) | collective-permute-done | bytes 841760 | tf_op jit(solution)/shard_map/ppermute | solution.py:19
  445.5 2.3 collective-permute-done.5
  448.8 7.5 %fusion.47 = (f32[6,137,20,2]{3,1,2,0:T(8,128)}, f32[6,137,20,2]{3,1,2,0:T(8,128)}) fusion(f32[6,137,20,128]{3,1,2,0:T(8,128)S(1)} %pad_maximum_fusion.1), kind=kLoop, calls=%fused_computation.117 | loop fusion | bytes 526080 | tf_op jit(solution)/shard_map/slice | solution.py:14
  456.2 7.2 %copy.27 = f32[6,137,20,2]{1,2,3,0:T(8,128)S(1)} copy(f32[6,137,20,2]{3,1,2,0:T(8,128)} %get-tuple-element.161) | data formatting | bytes 263040 | tf_op jit(solution)/shard_map/slice | solution.py:13
  463.5 1.3 collective-permute-start.6
  464.8 7.9 %copy.29 = f32[6,137,20,2]{1,2,3,0:T(8,128)} copy(f32[6,137,20,2]{3,1,2,0:T(8,128)} %get-tuple-element.160) | data formatting | bytes 263040 | tf_op jit(solution)/shard_map/slice | solution.py:14
  472.7 5.5 %collective-permute-start.7 = (f32[6,137,20,2]{1,2,3,0:T(8,128)}, f32[6,137,20,2]{1,2,3,0:T(8,128)}, u32[]{:S(2)}, u32[]{:S(2)}) collective-permute-start(f32[6,137,20,2]{1,2,3,0:T(8,128)} %copy.29), channel_id=1, source_target_pairs={{0,8},{8,16},{16,24},{1,9},{9,17},{17,25},{2,10},{10,18},{18,26},{... | collective-permute-start | bytes 394568 | tf_op jit(solution)/shard_map/ppermute | solution.py:17
  478.2 1.8 fusion.38
  480.1 6.1 %copy.28 = f32[6,137,20,2]{3,1,2,0:T(8,128)} copy(f32[6,137,20,2]{1,2,3,0:T(8,128)} %collective-permute-done.6) | data formatting | bytes 263040 | tf_op jit(solution)/shard_map/ppermute | solution.py:19
  486.1 6.0 %copy.30 = f32[6,137,20,2]{3,1,2,0:T(8,128)} copy(f32[6,137,20,2]{1,2,3,0:T(8,128)} %collective-permute-done.7) | data formatting | bytes 263040 | tf_op jit(solution)/shard_map/ppermute | solution.py:17
  492.1 35.5 %multiply_subtract_fusion = f32[6,137,16,128]{3,1,2,0:T(8,128)} fusion(f32[6,137,16,128]{3,1,2,0:T(8,128)} %multiply_subtract_fusion.1, f32[6,137,20,2]{3,1,2,0:T(8,128)} %copy.28, f32[6,137,2,128]{3,1,2,0:T(8,128)S(1)} %collective-permute-done.4, f32[6,137,2,128]{3,1,2,0:T(8,128)} %copy-done, f32[6,137,20,2]{3,1,2,0:T(8,128)} %copy.30, ...), kind=kLoop, calls=%fused_computation.87 | loop fusion | flops 69021696 | bytes 17658752 | tf_op jit(solution)/shard_map/sub | solution.py:76
  527.6 8.0 %copy.31 = f32[6,137,16,128]{3,2,1,0:T(8,128)} copy(f32[6,137,16,128]{3,1,2,0:T(8,128)} %multiply_subtract_fusion) | data formatting | bytes 13467648
  (123 shorter events, 34.7 us)
Async XLA Ops:
  68.1 3.8 copy-start.2
  225.2 17.3 %collective-permute-start = (f32[6,137,2,128]{3,1,2,0:T(8,128)S(1)}, f32[6,137,2,128]{3,1,2,0:T(8,128)S(1)}, u32[]{:S(2)}, u32[]{:S(2)}) collective-permute-start(f32[6,137,2,128]{3,1,2,0:T(8,128)S(1)} %get-tuple-element.171), channel_id=1, source_target_pairs={{1,0},{2,1},{3,2},{4,3},{5,4},{6,5},{7,6},{0,7},{9,8},{10,9},{11,1... | collective-permute-start | bytes 2525192 | tf_op jit(solution)/shard_map/ppermute | solution.py:19
  225.3 17.3 %collective-permute-start.1 = (f32[6,137,2,128]{3,1,2,0:T(8,128)S(1)}, f32[6,137,2,128]{3,1,2,0:T(8,128)S(1)}, u32[]{:S(2)}, u32[]{:S(2)}) collective-permute-start(f32[6,137,2,128]{3,1,2,0:T(8,128)S(1)} %get-tuple-element.170), channel_id=1, source_target_pairs={{0,1},{1,2},{2,3},{3,4},{4,5},{5,6},{6,7},{7,0},{8,9},{9,10},{10,1... | collective-permute-start | bytes 2525192 | tf_op jit(solution)/shard_map/ppermute | solution.py:17
  242.6 0.9 copy-start.1
  261.7 114.2 %collective-permute-start.2 = (f32[6,137,20,2]{1,2,3,0:T(8,128)S(1)}, f32[6,137,20,2]{1,2,3,0:T(8,128)}, u32[]{:S(2)}, u32[]{:S(2)}) collective-permute-start(f32[6,137,20,2]{1,2,3,0:T(8,128)S(1)} %copy.23), channel_id=1, source_target_pairs={{8,0},{16,8},{24,16},{9,1},{17,9},{25,17},{10,2},{18,10},{26,18},{... | collective-permute-start | bytes 394568 | tf_op jit(solution)/shard_map/ppermute | solution.py:19
  270.9 111.1 %collective-permute-start.3 = (f32[6,137,20,2]{1,2,3,0:T(8,128)}, f32[6,137,20,2]{1,2,3,0:T(8,128)}, u32[]{:S(2)}, u32[]{:S(2)}) collective-permute-start(f32[6,137,20,2]{1,2,3,0:T(8,128)} %copy.25), channel_id=1, source_target_pairs={{0,8},{8,16},{16,24},{1,9},{9,17},{17,25},{2,10},{10,18},{18,26},{... | collective-permute-start | bytes 394568 | tf_op jit(solution)/shard_map/ppermute | solution.py:17
  425.6 22.3 %slice-start = ((s8[7077888]{0:T(1024)(128)(4,1)}), s8[4194304]{0:T(1024)(128)(4,1)S(1)}, s32[]{:S(2)}) async-start(s8[7077888]{0:T(1024)(128)(4,1)} %bitcast.126), calls=%async_computation | async-start | bytes 8388608
  425.6 19.9 %collective-permute-start.4 = (f32[6,137,2,128]{3,1,2,0:T(8,128)S(1)}, f32[6,137,2,128]{3,1,2,0:T(8,128)S(1)}, u32[]{:S(2)}, u32[]{:S(2)}) collective-permute-start(f32[6,137,2,128]{3,1,2,0:T(8,128)S(1)} %get-tuple-element.167), channel_id=1, source_target_pairs={{1,0},{2,1},{3,2},{4,3},{5,4},{6,5},{7,6},{0,7},{9,8},{10,9},{11,1... | collective-permute-start | bytes 2525192 | tf_op jit(solution)/shard_map/ppermute | solution.py:19
  426.4 21.5 %collective-permute-start.5 = (f32[6,137,2,128]{3,1,2,0:T(8,128)S(1)}, f32[6,137,2,128]{3,1,2,0:T(8,128)S(1)}, u32[]{:S(2)}, u32[]{:S(2)}) collective-permute-start(f32[6,137,2,128]{3,1,2,0:T(8,128)S(1)} %get-tuple-element.166), channel_id=1, source_target_pairs={{0,1},{1,2},{2,3},{3,4},{4,5},{5,6},{6,7},{7,0},{8,9},{9,10},{10,1... | collective-permute-start | bytes 2525192 | tf_op jit(solution)/shard_map/ppermute | solution.py:17
  426.4 21.5 %slice-start.1 = ((s8[7077888]{0:T(1024)(128)(4,1)}), s8[2883584]{0:T(1024)(128)(4,1)S(1)}, s32[]{:S(2)}) async-start(s8[7077888]{0:T(1024)(128)(4,1)} %bitcast.126), calls=%async_computation.1 | async-start | bytes 5767168
  447.8 0.9 copy-start
  463.5 16.6 %collective-permute-start.6 = (f32[6,137,20,2]{1,2,3,0:T(8,128)S(1)}, f32[6,137,20,2]{1,2,3,0:T(8,128)}, u32[]{:S(2)}, u32[]{:S(2)}) collective-permute-start(f32[6,137,20,2]{1,2,3,0:T(8,128)S(1)} %copy.27), channel_id=1, source_target_pairs={{8,0},{16,8},{24,16},{9,1},{17,9},{25,17},{10,2},{18,10},{26,18},{... | collective-permute-start | bytes 394568 | tf_op jit(solution)/shard_map/ppermute | solution.py:19
  472.7 13.4 %collective-permute-start.7 = (f32[6,137,20,2]{1,2,3,0:T(8,128)}, f32[6,137,20,2]{1,2,3,0:T(8,128)}, u32[]{:S(2)}, u32[]{:S(2)}) collective-permute-start(f32[6,137,20,2]{1,2,3,0:T(8,128)} %copy.29), channel_id=1, source_target_pairs={{0,8},{8,16},{16,24},{1,9},{9,17},{17,25},{2,10},{10,18},{18,26},{... | collective-permute-start | bytes 394568 | tf_op jit(solution)/shard_map/ppermute | solution.py:17
where the time goes:
time: 541 us; the launch traced here: 536 us
  local copies, waits for them, and re-layouts  222 us (41%)
  other arithmetic  119 us (22%)
  starting transfers between devices  113 us (21%)
  matrix products  50 us (9%)
  waiting for transfers between devices  29.9 us (6%)
    ppermute x4, starting transfers between devices, padded(): lax.ppermute(tail, axis, [(i, (i + 1) % count) for i in range(ends)])  109 us
    sub x2, other arithmetic, advance(): center - 0.15 * (center[4] * along_x + center[5] * along_y) - 0.06 * hyper  71.6 us
    gather x2, local copies, waits for them, and re-layouts, physics_set(): placed = jnp.take(done, jnp.maximum(ranks, 0), axis=2, mode='clip')  36.7 us
    slice x6, local copies, waits for them, and re-layouts, padded(): lax.slice_in_dim(cells, cells.shape[dim] - width, cells.shape[dim], axis=...  34 us
    unnamed x13, local copies, waits for them, and re-layouts  29.3 us
    ppermute x4, waiting for transfers between devices, padded(): lax.ppermute(head, axis, [((i + 1) % count, i) for i in range(ends)])  27.6 us
    dot_general x8, matrix products, column_tend(): jnp.dot(w_hidden[0], hidden, preferred_element_type=jnp.float32)  26.9 us
    while x3, local copies, waits for them, and re-layouts, physics_set(): lax.fori_loop(0, blocks, one_block, jnp.zeros(cols.shape, jnp.float32))  25.7 us
  transfers between devices with their start and end apart: 8, of which 3 were waited for; matrix products, arithmetic and copies ran while one was open for 7% of the time, Pallas kernels for 0%

commit v1 on v0

v1 whole, which is shorter than its diff:
```python
import functools

import jax
import jax.numpy as jnp
from jax import lax
from jax.experimental import pallas as pl
from jax.experimental.pallas import tpu as pltpu
from jax.sharding import PartitionSpec as P

ITERS = 3
LANES = 128
HALO = 4
VMEM_LIMIT = 56 * 1024 * 1024


def silu(v):
    half = 0.5 * v
    return half + half * jnp.tanh(half)


def network(z, w_in, w_hidden, w_out, h_a, h_b, out):
    hid = w_in.shape[0]
    part = 256

    def layer(weight, source, target):
        for m in range(0, hid, part):
            acc = jnp.dot(weight(m), source, preferred_element_type=jnp.float32)
            target[m : m + part, :] = silu(acc).astype(jnp.bfloat16)

    layer(lambda m: w_in[m : m + part, :], z, h_a)
    layer(lambda m: w_hidden[0, m : m + part, :], h_a[...], h_b)
    layer(lambda m: w_hidden[1, m : m + part, :], h_b[...], h_a)
    out[: w_out.shape[0], :] = jnp.dot(w_out[...], h_a[...], preferred_element_type=jnp.float32)


def saturate(temp, vapour, water):
    temp0, vapour0, water0 = temp, vapour, water
    for _ in range(ITERS):
        satur = 0.5 * jnp.exp(0.5 * temp)
        delta = jnp.maximum(0.5 * (vapour - satur), -water)
        temp = temp + 0.5 * delta
        vapour = vapour - delta
        water = water + delta
    autoconv = 0.6 * jnp.maximum(water - 0.8, 0.0)
    water = water - autoconv
    return temp - temp0, vapour - vapour0, water - water0, autoconv


def physics_rows(rows, levels, lon, state, conv, micro, weights, scr, put):
    w_in, w_hidden, w_out = weights
    h_a, h_b, out = scr

    def field(f, l):
        return state[pl.ds(f * levels * lon + l, levels, stride=lon), :]

    z = jnp.concatenate(
        [state[pl.ds(l, 6 * levels, stride=lon), :].astype(jnp.bfloat16) for l in rows], axis=1
    )
    network(z, w_in, w_hidden, w_out, h_a, h_b, out)
    for k, l in enumerate(rows):
        c = conv[pl.ds(l, 1), :].astype(jnp.float32)
        m = micro[pl.ds(l, 1), :].astype(jnp.float32)
        cols = slice(k * LANES, (k + 1) * LANES)

        def net(f):
            return c * out[f * levels : (f + 1) * levels, cols]

        temp, vapour, water = field(0, l), field(1, l), field(2, l)
        d_t, d_q, d_w, auto = saturate(temp, vapour, water)
        t0 = net(0) + m * d_t
        put(k, 0, temp + t0, t0)
        t1 = net(1) + m * d_q
        put(k, 1, vapour + t1, t1)
        t2 = m * d_w
        put(k, 2, water + t2, t2)
        t3 = m * auto
        put(k, 3, field(3, l) + t3, t3)
        t4 = net(2)
        put(k, 4, field(4, l) + t4, t4)
        t5 = net(3)
        put(k, 5, field(5, l) + t5, t5)


def edge_kernel(levels, lon, state, conv, micro, w_in, w_hidden, w_out, lo, hi, tlo, thi, h_a, h_b, out):
    @pl.loop(0, HALO // 2)
    def _(i):
        rows = [2 * i, 2 * i + 1, lon - HALO + 2 * i, lon - HALO + 2 * i + 1]

        def put(k, f, upd, tend):
            u_ref, t_ref = (lo, tlo) if k < 2 else (hi, thi)
            u_ref[2 * i + k % 2, f, :levels, :] = upd
            t_ref[2 * i + k % 2, f, :levels, :] = tend

        physics_rows(rows, levels, lon, state, conv, micro, (w_in, w_hidden, w_out), (h_a, h_b, out), put)


def pack(tile, tiles, lane):
    acc = None
    for j in range(tiles):
        turned = pltpu.roll(tile(j), (8 * j + 4) % LANES, 1)
        acc = turned if acc is None else jnp.where(lane // 8 == j, turned, acc)
    return acc


def inner_kernel(
    levels, lon, groups, tiles, state, conv, micro, w_in, w_hidden, w_out, lo, hi, tlo, thi,
    mid, tend, packed, h_a, h_b, out,
):
    @pl.loop(0, (lon - 2 * HALO) // 4)
    def _(i):
        rows = [HALO + 4 * i + k for k in range(4)]

        def put(k, f, upd, tnd):
            mid[4 * i + k, f, :levels, :] = upd
            tend[pl.ds(f * levels * lon + rows[k], levels, stride=lon), :] = tnd

        physics_rows(rows, levels, lon, state, conv, micro, (w_in, w_hidden, w_out), (h_a, h_b, out), put)

    @pl.loop(0, HALO)
    def _(i):
        for f in range(6):
            tend[pl.ds(f * levels * lon + i, levels, stride=lon), :] = tlo[i, f, :levels, :]
            tend[pl.ds(f * levels * lon + lon - HALO + i, levels, stride=lon), :] = thi[i, f, :levels, :]

    lane = lax.broadcasted_iota(jnp.int32, (8, LANES), 1)
    for source, first, count in ((lo, 0, HALO), (mid, HALO, lon - 2 * HALO), (hi, lon - HALO, HALO)):

        @pl.loop(0, count)
        def _(i, source=source, first=first):
            for f in range(6):
                for g in range(groups):
                    packed[first + i, f, g] = pack(
                        lambda j: source[i, f, pl.ds((g * tiles + j) * 8, 8), :], tiles, lane
                    )


def stencil(center, xs, ys, u, v):
    xm2, xm1, xp1, xp2 = xs
    ym2, ym1, yp1, yp2 = ys
    along_x = 8.0 * (xp1 - xm1) - (xp2 - xm2)
    along_y = 8.0 * (yp1 - ym1) - (yp2 - ym2)
    one = (xp1 + xm1) + (yp1 + ym1)
    two = (xp2 + xm2) + (yp2 + ym2)
    return 0.28 * center + (u * along_x + v * along_y) + (0.24 * one - 0.06 * two)


def y_shifts(center, beyond, masks):
    low1, low2, high1, high2 = masks
    return (
        pltpu.roll(jnp.where(high2, beyond, center), 2, 1),
        pltpu.roll(jnp.where(high1, beyond, center), 1, 1),
        pltpu.roll(jnp.where(low1, beyond, center), LANES - 1, 1),
        pltpu.roll(jnp.where(low2, beyond, center), LANES - 2, 1),
    )


def advect_kernel(lon, tiles, left, lo, mid, hi, right, px, halo, inside, adv, px_l, px_r, s1_halo, s1):
    lane = lax.broadcasted_iota(jnp.int32, (8, LANES), 1)
    slot = lane % 8
    masks = (lane == 0, lane < 2, lane == LANES - 1, lane >= LANES - 2)
    slot_masks = (slot == 4, (slot == 4) | (slot == 5), slot == 3, (slot == 3) | (slot == 2))
    ext = lon + 2 * HALO
    scale = -0.15 / 12.0

    def place(r):
        for ref, first, count in (
            (left, 0, HALO),
            (lo, HALO, HALO),
            (mid, 2 * HALO, lon - 2 * HALO),
            (hi, lon, HALO),
            (right, lon + HALO, HALO),
        ):
            if r < first + count:
                return ref, r - first

    for ref, target, at in ((left, px_l, HALO - 2), (right, px_r, 0)):
        for i in range(2):

            @pl.loop(0, 6)
            def _(f, i=i, ref=ref, target=target, at=at):
                target[i, f] = pack(lambda j: ref[at + i, f, pl.ds(j * 8, 8), :], tiles, lane)

    def px_at(r, f):
        if r < HALO:
            return px_l[r - 2, f]
        if r >= lon + HALO:
            return px_r[r - lon - HALO, f]
        return px[r - HALO, f, 0]

    keep = inside[...]
    for r in range(2, ext - 2):
        u = scale * halo[r, 4, 0]
        v = scale * halo[r, 5, 0]

        @pl.loop(0, 6)
        def _(f, r=r, u=u, v=v):
            c = halo[r, f, 0]
            xs = [halo[r + d, f, 0] for d in (-2, -1, 1, 2)]
            ys = y_shifts(c, px_at(r, f), slot_masks)
            s1_halo[r - 2, f] = keep * stencil(c, xs, ys, u, v)

    @pl.loop(0, tiles)
    def _(t):
        rows = pl.ds(pl.multiple_of(t * 8, 8), 8)
        turn = LANES - (8 * t + 4)

        def at(r, f):
            ref, i = place(r)
            return ref[i, f, rows, :]

        for r in range(2, ext - 2):
            u = scale * at(r, 4)
            v = scale * at(r, 5)
            for f in range(6):
                c = at(r, f)
                xs = [at(r + d, f) for d in (-2, -1, 1, 2)]
                ys = y_shifts(c, pltpu.roll(halo[r, f, 0], turn, 1), masks)
                s1[r - 2, f] = stencil(c, xs, ys, u, v)
        for r in range(2, ext - 6):
            u = scale * s1[r, 4]
            v = scale * s1[r, 5]
            for f in range(6):
                c = s1[r, f]
                xs = [s1[r + d, f] for d in (-2, -1, 1, 2)]
                ys = y_shifts(c, pltpu.roll(s1_halo[r, f], turn, 1), masks)
                adv[f, pl.ds(t * (8 * lon) + (r - 2), 8, stride=lon), :] = stencil(c, xs, ys, u, v)


def local(state, conv_mask, micro_mask, w_in, w_hidden, w_out):
    fields, levels, lon, lat = state.shape
    hid = w_in.shape[0]
    groups = 2
    tiles = -(-levels // (8 * groups))
    pad = groups * tiles * 8
    flat = fields * levels * lon
    cells = state.reshape(flat, lat)
    f32 = jnp.float32
    full = pl.BlockSpec(memory_space=pltpu.VMEM)
    params = pltpu.CompilerParams(vmem_limit_bytes=VMEM_LIMIT)
    scratch = [
        pltpu.VMEM((hid, 4 * lat), jnp.bfloat16),
        pltpu.VMEM((hid, 4 * lat), jnp.bfloat16),
        pltpu.VMEM((-(-w_out.shape[0] // 8) * 8, 4 * lat), f32),
    ]

    def cost(rows):
        return pl.CostEstimate(
            flops=2 * rows * lat * (w_in.size + w_hidden.size + w_out.size),
            bytes_accessed=4 * flat * lat * 2 + 2 * (w_in.size + w_hidden.size + w_out.size),
            transcendentals=3 * rows * lat * (hid + levels),
        )

    edge = jax.ShapeDtypeStruct((HALO, fields, pad, lat), f32)
    lo, hi, tlo, thi = pl.pallas_call(
        functools.partial(edge_kernel, levels, lon),
        out_shape=[edge] * 4,
        in_specs=[full] * 6,
        out_specs=[full] * 4,
        scratch_shapes=scratch,
        compiler_params=params,
        cost_estimate=cost(2 * HALO),
        name="physics_edge",
    )(cells, conv_mask, micro_mask, w_in, w_hidden, w_out)

    def both(axis, up, down, closed):
        n = lax.axis_size(axis)
        ends = n if closed else n - 1
        return (
            lax.ppermute(up, axis, [(i, (i + 1) % n) for i in range(ends)]),
            lax.ppermute(down, axis, [((i + 1) % n, i) for i in range(ends)]),
        )

    left, right = both("col", hi, lo, True)
    mid, tend, px = pl.pallas_call(
        functools.partial(inner_kernel, levels, lon, groups, tiles),
        out_shape=[
            jax.ShapeDtypeStruct((lon - 2 * HALO, fields, pad, lat), f32),
            jax.ShapeDtypeStruct((flat, lat), f32),
            jax.ShapeDtypeStruct((lon, fields, groups, 8, lat), f32),
        ],
        in_specs=[full] * 10,
        out_specs=[full] * 3,
        scratch_shapes=scratch,
        compiler_params=params,
        cost_estimate=cost(lon - 2 * HALO),
        name="physics_inner",
    )(cells, conv_mask, micro_mask, w_in, w_hidden, w_out, lo, hi, tlo, thi)

    before, after = both("row", px, px, False)
    slot = lax.broadcasted_iota(jnp.int32, (8, lat), 1) % 8
    own = jnp.where(slot < 4, before, after)
    corner_l, corner_r = both("col", own[lon - HALO :], own[:HALO], True)
    halo = jnp.concatenate([corner_l, own, corner_r], axis=0)
    row = lax.axis_index("row")
    first, last = row == 0, row == lax.axis_size("row") - 1
    inside = jnp.where(jnp.where(slot < 4, first, last), 0.0, 1.0).astype(f32)

    ext = lon + 2 * HALO

    def rows_spec(n):
        return pl.BlockSpec((n, fields, 8 * tiles, lat), lambda g: (0, 0, g, 0))

    def packed_spec(n):
        return pl.BlockSpec((n, fields, 1, 8, lat), lambda g: (0, 0, g, 0, 0))

    adv = pl.pallas_call(
        functools.partial(advect_kernel, lon, tiles),
        grid=(groups,),
        out_shape=jax.ShapeDtypeStruct((fields, levels * lon, lat), f32),
        in_specs=[
            rows_spec(HALO),
            rows_spec(HALO),
            rows_spec(lon - 2 * HALO),
            rows_spec(HALO),
            rows_spec(HALO),
            packed_spec(lon),
            packed_spec(ext),
            pl.BlockSpec((8, lat), lambda g: (0, 0)),
        ],
        out_specs=pl.BlockSpec((fields, 8 * tiles * lon, lat), lambda g: (0, g, 0)),
        scratch_shapes=[
            pltpu.VMEM((2, fields, 8, lat), f32),
            pltpu.VMEM((2, fields, 8, lat), f32),
            pltpu.VMEM((ext - 4, fields, 8, lat), f32),
            pltpu.VMEM((ext - 4, fields, 8, lat), f32),
        ],
        compiler_params=params,
        cost_estimate=pl.CostEstimate(
            flops=60 * flat * lat, bytes_accessed=12 * flat * lat, transcendentals=0
        ),
        name="advect",
    )(left, lo, mid, hi, right, px, halo, inside)
    return adv.reshape(state.shape), tend.reshape(state.shape)


def solution(mesh):
    in_specs = (P(None, None, "col", "row"), P("col", "row"), P("col", "row"), P(), P(), P())
    out_specs = (P(None, None, "col", "row"), P(None, None, "col", "row"))
    return jax.shard_map(local, mesh=mesh, in_specs=in_specs, out_specs=out_specs, check_vma=False)
```

time: 541 us -> 383 us (0.71)
  the two profiles are of different devices: /device:TPU:0 before, /device:TPU:7 now
where the time goes in v1:
time: 383 us; the launch traced here: 382 us
  Pallas kernels  324 us (85%)
  waiting for transfers between devices  37.7 us (10%)
  starting transfers between devices  10.8 us (3%)
  local copies, waits for them, and re-layouts  5.59 us (1%)
    pallas_call x1, Pallas kernels, local(): pl.pallas_call(functools.partial(advect_kernel, lon, tiles), grid=(groups...  278 us
    pallas_call x1, Pallas kernels, local(): pl.pallas_call(functools.partial(inner_kernel, levels, lon, groups, tiles...  27.7 us
    ppermute x3, waiting for transfers between devices, both(): lax.ppermute(up, axis, [(i, (i + 1) % n) for i in range(ends)])  21.4 us
    pallas_call x1, Pallas kernels, local(): pl.pallas_call(functools.partial(edge_kernel, levels, lon), out_shape=[ed...  18.9 us
    ppermute x3, waiting for transfers between devices, both(): lax.ppermute(down, axis, [((i + 1) % n, i) for i in range(ends)])  16.4 us
  transfers between devices with their start and end apart: 6, of which 4 were waited for; matrix products, arithmetic and copies ran while one was open for 1% of the time, Pallas kernels for 7%

profile of v1, /device:TPU:7, one launch (start us, length us, event | category | flops | bytes accessed | tf_op | source)
XLA Modules:
  0.0 382.4 jit_solution(9156450623324200442)
XLA Ops:
  0.6 3.7 copy.8.w_in
  4.4 18.9 %physics_edge.1 = (f32[4,6,144,128]{3,2,1,0:T(8,128)}, f32[4,6,144,128]{3,2,1,0:T(8,128)}, f32[4,6,144,128]{3,2,1,0:T(8,128)}, f32[4,6,144,128]{3,2,1,0:T(8,128)}) custom-call(f32[13152,128]{1,0:T(8,128)} %bitcast.4, s32[16,128]{1,0:T(8,128)} %conv.3, s32[16,128]{1,0:T(8,128)} %micro.3, bf16[1024,822]{1,0:T(8,128)(2,1)} %copy.8.w_in, ...), custom_call_target="tpu_custom_call" | custom-call | flops 7168065536 | bytes 20467712 | tf_op jit(solution)/shard_map/physics_edge/pallas_call | solution.py:254
  23.3 1.9 collective-permute-start
  25.1 0.0 collective-permute-start.1
  25.1 27.7 %physics_inner.1 = (f32[8,6,144,128]{3,2,1,0:T(8,128)}, f32[13152,128]{1,0:T(8,128)}, f32[16,6,2,8,128]{4,3,2,1,0:T(8,128)}) custom-call(f32[13152,128]{1,0:T(8,128)} %bitcast.5, s32[16,128]{1,0:T(8,128)} %conv.3, s32[16,128]{1,0:T(8,128)} %micro.3, bf16[1024,822]{1,0:T(8,128)(2,1)} %copy.8.w_in, bf16[2,1024,1024]{2,1,0:T(8,128)(2,1)} %w_hidden.3, ...), custom_call_target="tpu_custom_call" | custom-call | flops 7168065536 | bytes 20467712 | tf_op jit(solution)/shard_map/physics_inner/pallas_call | solution.py:274
  52.8 3.1 collective-permute-start.3
  56.0 1.3 collective-permute-start.2
  57.3 0.6 select_select_fusion
  57.9 11.9 %collective-permute-done.3 = f32[16,6,2,8,128]{4,3,2,1,0:T(8,128)} collective-permute-done((f32[16,6,2,8,128]{4,3,2,1,0:T(8,128)}, f32[16,6,2,8,128]{4,3,2,1,0:T(8,128)}, u32[]{:S(2)}, u32[]{:S(2)}) %collective-permute-start.3) | collective-permute-done | bytes 786464 | tf_op jit(solution)/shard_map/ppermute | solution.py:270
  69.8 18.7 %collective-permute-done.2 = f32[16,6,2,8,128]{4,3,2,1,0:T(8,128)} collective-permute-done((f32[16,6,2,8,128]{4,3,2,1,0:T(8,128)}, f32[16,6,2,8,128]{4,3,2,1,0:T(8,128)}, u32[]{:S(2)}, u32[]{:S(2)}) %collective-permute-start.2) | collective-permute-done | bytes 786464 | tf_op jit(solution)/shard_map/ppermute | solution.py:269
  88.5 1.5 broadcast_select_fusion
  90.0 4.5 %collective-permute-start.4 = (f32[4,6,2,8,128]{4,3,2,1,0:T(8,128)S(1)}, f32[4,6,2,8,128]{4,3,2,1,0:T(8,128)S(1)}, u32[]{:S(2)}, u32[]{:S(2)}) collective-permute-start(f32[4,6,2,8,128]{4,3,2,1,0:T(8,128)S(1)} %get-tuple-element.18), channel_id=1, source_target_pairs={{0,1},{1,2},{2,3},{3,4},{4,5},{5,6},{6,7},{7,0},{8,9},{9,10},{10,1... | collective-permute-start | bytes 589832 | tf_op jit(solution)/shard_map/ppermute | solution.py:269
  94.5 0.0 collective-permute-start.5
  94.5 2.6 collective-permute-done.4
  97.2 4.5 %collective-permute-done.5 = f32[4,6,2,8,128]{4,3,2,1,0:T(8,128)S(1)} collective-permute-done((f32[4,6,2,8,128]{4,3,2,1,0:T(8,128)S(1)}, f32[4,6,2,8,128]{4,3,2,1,0:T(8,128)S(1)}, u32[]{:S(2)}, u32[]{:S(2)}) %collective-permute-start.5) | collective-permute-done | bytes 196640 | tf_op jit(solution)/shard_map/ppermute | solution.py:270
  101.7 1.1 pad_maximum_fusion.halo
  102.8 0.0 collective-permute-done.left
  102.8 0.0 copy-start
  102.8 0.0 collective-permute-done.1.right
  102.8 0.0 copy-start.1
  102.8 1.3 copy-done
  104.1 0.5 copy-done.1
  104.6 277.8 %advect.1 = f32[6,2192,128]{2,1,0:T(8,128)} custom-call(f32[4,6,144,128]{3,2,1,0:T(8,128)} %copy-done, f32[4,6,144,128]{3,2,1,0:T(8,128)} %get-tuple-element.10.lo, f32[8,6,144,128]{3,2,1,0:T(8,128)} %get-tuple-element.13.mid, f32[4,6,144,128]{3,2,1,0:T(8,128)} %get-tuple-element.9.hi, f32[4,6,144,128]{3,2,1,0:T(8,128)} %copy-done.1, ...), custom_call_target="tpu_custom_call" | custom-call | flops 101007360 | bytes 20201472 | tf_op jit(solution)/shard_map/advect/pallas_call | solution.py:306
  (3 shorter events, 0.0 us)
Async XLA Ops:
  23.3 79.5 %collective-permute-start = (f32[4,6,144,128]{3,2,1,0:T(8,128)}, f32[4,6,144,128]{3,2,1,0:T(8,128)S(1)}, u32[]{:S(2)}, u32[]{:S(2)}) collective-permute-start(f32[4,6,144,128]{3,2,1,0:T(8,128)} %get-tuple-element.9.hi), channel_id=1, source_target_pairs={{0,1},{1,2},{2,3},{3,4},{4,5},{5,6},{6,7},{7,0},{8,9},{9,10},{10,1... | collective-permute-start | bytes 5308424 | tf_op jit(solution)/shard_map/ppermute | solution.py:269
  25.1 77.6 %collective-permute-start.1 = (f32[4,6,144,128]{3,2,1,0:T(8,128)}, f32[4,6,144,128]{3,2,1,0:T(8,128)S(1)}, u32[]{:S(2)}, u32[]{:S(2)}) collective-permute-start(f32[4,6,144,128]{3,2,1,0:T(8,128)} %get-tuple-element.10.lo), channel_id=1, source_target_pairs={{1,0},{2,1},{3,2},{4,3},{5,4},{6,5},{7,6},{0,7},{9,8},{10,9},{11,1... | collective-permute-start | bytes 5308424 | tf_op jit(solution)/shard_map/ppermute | solution.py:270
  52.8 16.9 %collective-permute-start.3 = (f32[16,6,2,8,128]{4,3,2,1,0:T(8,128)}, f32[16,6,2,8,128]{4,3,2,1,0:T(8,128)}, u32[]{:S(2)}, u32[]{:S(2)}) collective-permute-start(f32[16,6,2,8,128]{4,3,2,1,0:T(8,128)} %get-tuple-element.14.px), channel_id=1, source_target_pairs={{8,0},{16,8},{24,16},{9,1},{17,9},{25,17},{10,2},{18,10},{26,18},{... | collective-permute-start | bytes 2359304 | tf_op jit(solution)/shard_map/ppermute | solution.py:270
  56.0 32.5 %collective-permute-start.2 = (f32[16,6,2,8,128]{4,3,2,1,0:T(8,128)}, f32[16,6,2,8,128]{4,3,2,1,0:T(8,128)}, u32[]{:S(2)}, u32[]{:S(2)}) collective-permute-start(f32[16,6,2,8,128]{4,3,2,1,0:T(8,128)} %get-tuple-element.14.px), channel_id=1, source_target_pairs={{0,8},{8,16},{16,24},{1,9},{9,17},{17,25},{2,10},{10,18},{18,26},{... | collective-permute-start | bytes 2359304 | tf_op jit(solution)/shard_map/ppermute | solution.py:269
  90.0 7.1 %collective-permute-start.4 = (f32[4,6,2,8,128]{4,3,2,1,0:T(8,128)S(1)}, f32[4,6,2,8,128]{4,3,2,1,0:T(8,128)S(1)}, u32[]{:S(2)}, u32[]{:S(2)}) collective-permute-start(f32[4,6,2,8,128]{4,3,2,1,0:T(8,128)S(1)} %get-tuple-element.18), channel_id=1, source_target_pairs={{0,1},{1,2},{2,3},{3,4},{4,5},{5,6},{6,7},{7,0},{8,9},{9,10},{10,1... | collective-permute-start | bytes 589832 | tf_op jit(solution)/shard_map/ppermute | solution.py:269
  94.5 7.1 %collective-permute-start.5 = (f32[4,6,2,8,128]{4,3,2,1,0:T(8,128)S(1)}, f32[4,6,2,8,128]{4,3,2,1,0:T(8,128)S(1)}, u32[]{:S(2)}, u32[]{:S(2)}) collective-permute-start(f32[4,6,2,8,128]{4,3,2,1,0:T(8,128)S(1)} %get-tuple-element.19), channel_id=1, source_target_pairs={{1,0},{2,1},{3,2},{4,3},{5,4},{6,5},{7,6},{0,7},{9,8},{10,9},{11,1... | collective-permute-start | bytes 589832 | tf_op jit(solution)/shard_map/ppermute | solution.py:270
  102.8 1.3 copy-start
  102.8 1.8 copy-start.1

commit v2 on v1

--- a/solution.py
+++ b/solution.py
@@ -2,6 +2,7 @@
 
 import jax
 import jax.numpy as jnp
+import numpy as np
 from jax import lax
 from jax.experimental import pallas as pl
 from jax.experimental.pallas import tpu as pltpu
@@ -23,9 +24,14 @@
     part = 256
 
     def layer(weight, source, target):
-        for m in range(0, hid, part):
-            acc = jnp.dot(weight(m), source, preferred_element_type=jnp.float32)
-            target[m : m + part, :] = silu(acc).astype(jnp.bfloat16)
+        ready = None
+        for m in range(0, hid + part, part):
+            acc = None
+            if m < hid:
+                acc = jnp.dot(weight(m), source, preferred_element_type=jnp.float32)
+            if ready is not None:
+                target[m - part : m, :] = silu(ready).astype(jnp.bfloat16)
+            ready = acc
 
     layer(lambda m: w_in[m : m + part, :], z, h_a)
     layer(lambda m: w_hidden[0, m : m + part, :], h_a[...], h_b)
@@ -84,11 +90,13 @@
 def edge_kernel(levels, lon, state, conv, micro, w_in, w_hidden, w_out, lo, hi, tlo, thi, h_a, h_b, out):
     @pl.loop(0, HALO // 2)
     def _(i):
+        blank = jnp.zeros((lo.shape[2] - levels, LANES), jnp.float32)
         rows = [2 * i, 2 * i + 1, lon - HALO + 2 * i, lon - HALO + 2 * i + 1]
 
         def put(k, f, upd, tend):
             u_ref, t_ref = (lo, tlo) if k < 2 else (hi, thi)
             u_ref[2 * i + k % 2, f, :levels, :] = upd
+            u_ref[2 * i + k % 2, f, levels:, :] = blank
             t_ref[2 * i + k % 2, f, :levels, :] = tend
 
         physics_rows(rows, levels, lon, state, conv, micro, (w_in, w_hidden, w_out), (h_a, h_b, out), put)
@@ -109,9 +117,11 @@
     @pl.loop(0, (lon - 2 * HALO) // 4)
     def _(i):
         rows = [HALO + 4 * i + k for k in range(4)]
+        blank = jnp.zeros((mid.shape[2] - levels, LANES), jnp.float32)
 
         def put(k, f, upd, tnd):
             mid[4 * i + k, f, :levels, :] = upd
+            mid[4 * i + k, f, levels:, :] = blank
             tend[pl.ds(f * levels * lon + rows[k], levels, stride=lon), :] = tnd
 
         physics_rows(rows, levels, lon, state, conv, micro, (w_in, w_hidden, w_out), (h_a, h_b, out), put)
@@ -134,33 +144,59 @@
                     )
 
 
-def stencil(center, xs, ys, u, v):
+def split(x):
+    high = x.astype(jnp.bfloat16)
+    low = (x - high.astype(jnp.float32)).astype(jnp.bfloat16)
+    return jnp.concatenate([high, low], axis=-1)
+
+
+def banded(source, target):
+    dist = source[:, None] - target[None, :]
+    slope = 8.0 * (dist == 1) - 8.0 * (dist == -1) - 1.0 * (dist == 2) + 1.0 * (dist == -2)
+    hyper = 4.0 * (abs(dist) == 1) - 1.0 * (abs(dist) == 2) - 12.0 * (dist == 0)
+    half = np.concatenate([slope, hyper], axis=1)
+    return half
+
+
+def twice(half):
+    return np.concatenate([half, half], axis=0).astype(jnp.bfloat16)
+
+
+def matrices(lat, tiles):
+    lanes = np.arange(lat)
+    slot, group = lanes % 8, lanes // 8
+    beyond = np.where(slot < 4, slot - 4, lat + slot - 4)
+    own = np.where(slot < 4, lat + slot - 4, slot - 4)
+    center = twice(banded(lanes, lanes))
+    edges = np.stack([twice(banded(beyond, lanes) * (group == j)[:, None]) for j in range(tiles)])
+    same = np.concatenate([group[:, None] == group[None, :]] * 2, axis=1)
+    return center, edges, twice(banded(beyond, beyond) * same), twice(banded(own, beyond) * same)
+
+
+def stencil(center, xs, y, wind_u, wind_v):
     xm2, xm1, xp1, xp2 = xs
-    ym2, ym1, yp1, yp2 = ys
     along_x = 8.0 * (xp1 - xm1) - (xp2 - xm2)
-    along_y = 8.0 * (yp1 - ym1) - (yp2 - ym2)
-    one = (xp1 + xm1) + (yp1 + ym1)
-    two = (xp2 + xm2) + (yp2 + ym2)
-    return 0.28 * center + (u * along_x + v * along_y) + (0.24 * one - 0.06 * two)
-
-
-def y_shifts(center, beyond, masks):
-    low1, low2, high1, high2 = masks
-    return (
-        pltpu.roll(jnp.where(high2, beyond, center), 2, 1),
-        pltpu.roll(jnp.where(high1, beyond, center), 1, 1),
-        pltpu.roll(jnp.where(low1, beyond, center), LANES - 1, 1),
-        pltpu.roll(jnp.where(low2, beyond, center), LANES - 2, 1),
-    )
-
-
-def advect_kernel(lon, tiles, left, lo, mid, hi, right, px, halo, inside, adv, px_l, px_r, s1_halo, s1):
+    hyper = 4.0 * (xp1 + xm1) - (xp2 + xm2) + y[:, LANES:]
+    return center + (wind_u * along_x + wind_v * y[:, :LANES]) + 0.06 * hyper
+
+
+def winds(center):
+    scale = -0.15 / 12.0
+    u, v = scale * center[32:40], scale * center[40:48]
+    return jnp.concatenate([u] * 6, axis=0), jnp.concatenate([v] * 6, axis=0)
+
+
+def dot(a, b):
+    return jnp.dot(a, b, preferred_element_type=jnp.float32)
+
+
+def advect_kernel(
+    lon, tiles, left, lo, mid, hi, right, px, halo, inside, m_center, m_edges, m_packed, m_own, adv,
+    px_side, halo_parts, s1_parts, y, s1,
+):
     lane = lax.broadcasted_iota(jnp.int32, (8, LANES), 1)
-    slot = lane % 8
-    masks = (lane == 0, lane < 2, lane == LANES - 1, lane >= LANES - 2)
-    slot_masks = (slot == 4, (slot == 4) | (slot == 5), slot == 3, (slot == 3) | (slot == 2))
     ext = lon + 2 * HALO
-    scale = -0.15 / 12.0
+    n = 48
 
     def place(r):
         for ref, first, count in (
@@ -173,57 +209,51 @@
             if r < first + count:
                 return ref, r - first
 
-    for ref, target, at in ((left, px_l, HALO - 2), (right, px_r, 0)):
-        for i in range(2):
-
-            @pl.loop(0, 6)
-            def _(f, i=i, ref=ref, target=target, at=at):
-                target[i, f] = pack(lambda j: ref[at + i, f, pl.ds(j * 8, 8), :], tiles, lane)
-
-    def px_at(r, f):
-        if r < HALO:
-            return px_l[r - 2, f]
-        if r >= lon + HALO:
-            return px_r[r - lon - HALO, f]
-        return px[r - HALO, f, 0]
-
-    keep = inside[...]
+    for k, (ref, i) in enumerate(((left, 2), (left, 3), (right, 0), (right, 1))):
+
+        @pl.loop(0, 6)
+        def _(f, i=i, k=k, ref=ref):
+            px_side[k, f] = pack(lambda j: ref[i, f, pl.ds(j * 8, 8), :], tiles, lane)
+
+    def rows_of(a):
+        return a.reshape(-1, LANES)
+
+    beyond = rows_of(halo[...])
+    halo_parts[...] = split(beyond)
+    own = jnp.concatenate([rows_of(px_side[:2]), rows_of(px[...]), rows_of(px_side[2:])], axis=0)
+    y[...] = dot(halo_parts[2 * n : (ext - 2) * n, :], m_packed[...]) + dot(split(own), m_own[...])
+    keep = jnp.concatenate([inside[...]] * 6, axis=0)
     for r in range(2, ext - 2):
-        u = scale * halo[r, 4, 0]
-        v = scale * halo[r, 5, 0]
-
-        @pl.loop(0, 6)
-        def _(f, r=r, u=u, v=v):
-            c = halo[r, f, 0]
-            xs = [halo[r + d, f, 0] for d in (-2, -1, 1, 2)]
-            ys = y_shifts(c, px_at(r, f), slot_masks)
-            s1_halo[r - 2, f] = keep * stencil(c, xs, ys, u, v)
+        c = rows_of(halo[r])
+        xs = [rows_of(halo[r + d]) for d in (-2, -1, 1, 2)]
+        new = keep * stencil(c, xs, y[(r - 2) * n : (r - 1) * n, :], *winds(c))
+        s1_parts[(r - 2) * n : (r - 1) * n, :] = split(new)
 
     @pl.loop(0, tiles)
     def _(t):
         rows = pl.ds(pl.multiple_of(t * 8, 8), 8)
-        turn = LANES - (8 * t + 4)
-
-        def at(r, f):
+
+        def at(r):
             ref, i = place(r)
-            return ref[i, f, rows, :]
-
+            return rows_of(ref[i, :, rows, :])
+
+        cells = jnp.concatenate([at(r) for r in range(2, ext - 2)], axis=0)
+        y[...] = dot(split(cells), m_center[...]) + dot(halo_parts[2 * n : (ext - 2) * n, :], m_edges[t])
         for r in range(2, ext - 2):
-            u = scale * at(r, 4)
-            v = scale * at(r, 5)
+            c = at(r)
+            xs = [at(r + d) for d in (-2, -1, 1, 2)]
+            k = r - 2
+            s1[k * n : (k + 1) * n, :] = stencil(c, xs, y[k * n : (k + 1) * n, :], *winds(c))
+        last = lon * n
+        y[:last, :] = dot(split(s1[2 * n : 2 * n + last, :]), m_center[...]) + dot(
+            s1_parts[2 * n : 2 * n + last, :], m_edges[t]
+        )
+        for r in range(lon):
+            c = s1[(r + 2) * n : (r + 3) * n, :]
+            xs = [s1[(r + 2 + d) * n : (r + 3 + d) * n, :] for d in (-2, -1, 1, 2)]
+            new = stencil(c, xs, y[r * n : (r + 1) * n, :], *winds(c))
             for f in range(6):
-                c = at(r, f)
-                xs = [at(r + d, f) for d in (-2, -1, 1, 2)]
-                ys = y_shifts(c, pltpu.roll(halo[r, f, 0], turn, 1), masks)
-                s1[r - 2, f] = stencil(c, xs, ys, u, v)
-        for r in range(2, ext - 6):
-            u = scale * s1[r, 4]
-            v = scale * s1[r, 5]
-            for f in range(6):
-                c = s1[r, f]
-                xs = [s1[r + d, f] for d in (-2, -1, 1, 2)]
-                ys = y_shifts(c, pltpu.roll(s1_halo[r, f], turn, 1), masks)
-                adv[f, pl.ds(t * (8 * lon) + (r - 2), 8, stride=lon), :] = stencil(c, xs, ys, u, v)
+                adv[f, pl.ds(t * (8 * lon) + r, 8, stride=lon), :] = new[8 * f : 8 * f + 8]
 
 
 def local(state, conv_mask, micro_mask, w_in, w_hidden, w_out):
@@ -296,6 +326,7 @@
     inside = jnp.where(jnp.where(slot < 4, first, last), 0.0, 1.0).astype(f32)
 
     ext = lon + 2 * HALO
+    center, edges, packed, own_edges = (jnp.asarray(m) for m in matrices(lat, tiles))
 
     def rows_spec(n):
         return pl.BlockSpec((n, fields, 8 * tiles, lat), lambda g: (0, 0, g, 0))
@@ -316,20 +347,25 @@
             packed_spec(lon),
             packed_spec(ext),
             pl.BlockSpec((8, lat), lambda g: (0, 0)),
+            pl.BlockSpec(center.shape, lambda g: (0, 0)),
+            pl.BlockSpec(edges.shape, lambda g: (0, 0, 0)),
+            pl.BlockSpec(packed.shape, lambda g: (0, 0)),
+            pl.BlockSpec(own_edges.shape, lambda g: (0, 0)),
         ],
         out_specs=pl.BlockSpec((fields, 8 * tiles * lon, lat), lambda g: (0, g, 0)),
         scratch_shapes=[
-            pltpu.VMEM((2, fields, 8, lat), f32),
-            pltpu.VMEM((2, fields, 8, lat), f32),
-            pltpu.VMEM((ext - 4, fields, 8, lat), f32),
-            pltpu.VMEM((ext - 4, fields, 8, lat), f32),
+            pltpu.VMEM((4, fields, 8, lat), f32),
+            pltpu.VMEM((ext * 48, 2 * lat), jnp.bfloat16),
+            pltpu.VMEM(((ext - 4) * 48, 2 * lat), jnp.bfloat16),
+            pltpu.VMEM(((ext - 4) * 48, 2 * lat), f32),
+            pltpu.VMEM(((ext - 4) * 48, lat), f32),
         ],
         compiler_params=params,
         cost_estimate=pl.CostEstimate(
             flops=60 * flat * lat, bytes_accessed=12 * flat * lat, transcendentals=0
         ),
         name="advect",
-    )(left, lo, mid, hi, right, px, halo, inside)
+    )(left, lo, mid, hi, right, px, halo, inside, center, edges, packed, own_edges)
     return adv.reshape(state.shape), tend.reshape(state.shape)
 
 

time: 383 us -> 132 us (0.34)
  the two profiles are of different devices: /device:TPU:7 before, /device:TPU:5 now
where the time goes in v2:
time: 132 us
  Pallas kernels  74.3 us (56%)
  waiting for transfers between devices  36.4 us (28%)
  starting transfers between devices  12.1 us (9%)
  local copies, waits for them, and re-layouts  5.59 us (4%)
  other arithmetic  3.18 us (2%)
    pallas_call x1, Pallas kernels, local(): pl.pallas_call(functools.partial(inner_kernel, levels, lon, groups, tiles...  27.9 us
    pallas_call x1, Pallas kernels, local(): pl.pallas_call(functools.partial(advect_kernel, lon, tiles), grid=(groups...  27.2 us
    ppermute x3, waiting for transfers between devices, both(): lax.ppermute(up, axis, [(i, (i + 1) % n) for i in range(ends)])  19.9 us
    pallas_call x1, Pallas kernels, local(): pl.pallas_call(functools.partial(edge_kernel, levels, lon), out_shape=[ed...  19.1 us
    ppermute x3, waiting for transfers between devices, both(): lax.ppermute(down, axis, [((i + 1) % n, i) for i in range(ends)])  16.5 us
    ppermute x3, starting transfers between devices, both(): lax.ppermute(up, axis, [(i, (i + 1) % n) for i in range(ends)])  9.06 us
    unnamed x5, local copies, waits for them, and re-layouts  5.56 us
    ppermute x3, starting transfers between devices, both(): lax.ppermute(down, axis, [((i + 1) % n, i) for i in range(ends)])  3.06 us
  transfers between devices with their start and end apart: 6, of which 4 were waited for; matrix products, arithmetic and copies ran while one was open for 2% of the time, Pallas kernels for 21%

profile of v2, /device:TPU:5, one launch (start us, length us, event | category | flops | bytes accessed | tf_op | source)
XLA Modules:
  0.0 132.2 jit_solution(13607214254543559632)
XLA Ops:
  0.6 3.7 %copy.12.w_in = bf16[1024,822]{1,0:T(8,128)(2,1)} copy(bf16[1024,822]{0,1:T(8,128)(2,1)} %param.13) | data formatting | bytes 3366912 | tf_op args[3]
  4.4 19.1 %physics_edge.1 = (f32[4,6,144,128]{3,2,1,0:T(8,128)}, f32[4,6,144,128]{3,2,1,0:T(8,128)}, f32[4,6,144,128]{3,2,1,0:T(8,128)}, f32[4,6,144,128]{3,2,1,0:T(8,128)}) custom-call(f32[13152,128]{1,0:T(8,128)} %bitcast.4, s32[16,128]{1,0:T(8,128)} %conv.3, s32[16,128]{1,0:T(8,128)} %micro.3, bf16[1024,822]{1,0:T(8,128)(2,1)} %copy.12.w_in, ...), custom_call_target="tpu_custom_call" | custom-call | flops 7168065536 | bytes 20467712 | tf_op jit(solution)/shard_map/physics_edge/pallas_call | solution.py:284
  23.5 1.9 %collective-permute-start = (f32[4,6,144,128]{3,2,1,0:T(8,128)}, f32[4,6,144,128]{3,2,1,0:T(8,128)S(1)}, u32[]{:S(2)}, u32[]{:S(2)}) collective-permute-start(f32[4,6,144,128]{3,2,1,0:T(8,128)} %get-tuple-element.9.hi), channel_id=1, source_target_pairs={{0,1},{1,2},{2,3},{3,4},{4,5},{5,6},{6,7},{7,0},{8,9},{9,10},{10,1... | collective-permute-start | bytes 5308424 | tf_op jit(solution)/shard_map/ppermute | solution.py:299
  25.3 0.0 collective-permute-start.1
  25.3 27.9 %physics_inner.1 = (f32[8,6,144,128]{3,2,1,0:T(8,128)}, f32[13152,128]{1,0:T(8,128)}, f32[16,6,2,8,128]{4,3,2,1,0:T(8,128)}) custom-call(f32[13152,128]{1,0:T(8,128)} %bitcast.5, s32[16,128]{1,0:T(8,128)} %conv.3, s32[16,128]{1,0:T(8,128)} %micro.3, bf16[1024,822]{1,0:T(8,128)(2,1)} %copy.12.w_in, bf16[2,1024,1024]{2,1,0:T(8,128)(2,1)} %w_hidden.3, ...), custom_call_target="tpu_custom_call" | custom-call | flops 7168065536 | bytes 20467712 | tf_op jit(solution)/shard_map/physics_inner/pallas_call | solution.py:304
  53.2 3.0 %collective-permute-start.3 = (f32[16,6,2,8,128]{4,3,2,1,0:T(8,128)}, f32[16,6,2,8,128]{4,3,2,1,0:T(8,128)}, u32[]{:S(2)}, u32[]{:S(2)}) collective-permute-start(f32[16,6,2,8,128]{4,3,2,1,0:T(8,128)} %get-tuple-element.14.px), channel_id=1, source_target_pairs={{8,0},{16,8},{24,16},{9,1},{17,9},{25,17},{10,2},{18,10},{26,18},{... | collective-permute-start | bytes 2359304 | tf_op jit(solution)/shard_map/ppermute | solution.py:300
  56.3 3.2 %collective-permute-start.2 = (f32[16,6,2,8,128]{4,3,2,1,0:T(8,128)}, f32[16,6,2,8,128]{4,3,2,1,0:T(8,128)}, u32[]{:S(2)}, u32[]{:S(2)}) collective-permute-start(f32[16,6,2,8,128]{4,3,2,1,0:T(8,128)} %get-tuple-element.14.px), channel_id=1, source_target_pairs={{0,8},{8,16},{16,24},{1,9},{9,17},{17,25},{2,10},{10,18},{18,26},{... | collective-permute-start | bytes 2359304 | tf_op jit(solution)/shard_map/ppermute | solution.py:299
  59.5 0.6 select_select_fusion
  60.1 12.0 %collective-permute-done.3 = f32[16,6,2,8,128]{4,3,2,1,0:T(8,128)} collective-permute-done((f32[16,6,2,8,128]{4,3,2,1,0:T(8,128)}, f32[16,6,2,8,128]{4,3,2,1,0:T(8,128)}, u32[]{:S(2)}, u32[]{:S(2)}) %collective-permute-start.3) | collective-permute-done | bytes 786464 | tf_op jit(solution)/shard_map/ppermute | solution.py:300
  72.1 17.3 %collective-permute-done.2 = f32[16,6,2,8,128]{4,3,2,1,0:T(8,128)} collective-permute-done((f32[16,6,2,8,128]{4,3,2,1,0:T(8,128)}, f32[16,6,2,8,128]{4,3,2,1,0:T(8,128)}, u32[]{:S(2)}, u32[]{:S(2)}) %collective-permute-start.2) | collective-permute-done | bytes 786464 | tf_op jit(solution)/shard_map/ppermute | solution.py:299
  89.4 1.5 %broadcast_select_fusion = f32[16,6,2,8,128]{4,3,2,1,0:T(8,128)S(1)} fusion(f32[16,6,2,8,128]{4,3,2,1,0:T(8,128)} %collective-permute-done.2, f32[16,6,2,8,128]{4,3,2,1,0:T(8,128)} %collective-permute-done.3, pred[8,128]{1,0:T(8,128)(4,1)S(1)} %get-tuple-element.17), kind=kLoop, calls=%fused_computation.1 | loop fusion | flops 196608 | bytes 2360320 | tf_op jit(solution)/shard_map/jit(_where)/select_n | solution.py:321
  90.9 4.0 %collective-permute-start.4 = (f32[4,6,2,8,128]{4,3,2,1,0:T(8,128)S(1)}, f32[4,6,2,8,128]{4,3,2,1,0:T(8,128)S(1)}, u32[]{:S(2)}, u32[]{:S(2)}) collective-permute-start(f32[4,6,2,8,128]{4,3,2,1,0:T(8,128)S(1)} %get-tuple-element.18), channel_id=1, source_target_pairs={{0,1},{1,2},{2,3},{3,4},{4,5},{5,6},{6,7},{7,0},{8,9},{9,10},{10,1... | collective-permute-start | bytes 589832 | tf_op jit(solution)/shard_map/ppermute | solution.py:299
  94.9 0.0 collective-permute-start.5
  94.9 2.6 %collective-permute-done.4 = f32[4,6,2,8,128]{4,3,2,1,0:T(8,128)S(1)} collective-permute-done((f32[4,6,2,8,128]{4,3,2,1,0:T(8,128)S(1)}, f32[4,6,2,8,128]{4,3,2,1,0:T(8,128)S(1)}, u32[]{:S(2)}, u32[]{:S(2)}) %collective-permute-start.4) | collective-permute-done | bytes 196640 | tf_op jit(solution)/shard_map/ppermute | solution.py:299
  97.6 4.5 %collective-permute-done.5 = f32[4,6,2,8,128]{4,3,2,1,0:T(8,128)S(1)} collective-permute-done((f32[4,6,2,8,128]{4,3,2,1,0:T(8,128)S(1)}, f32[4,6,2,8,128]{4,3,2,1,0:T(8,128)S(1)}, u32[]{:S(2)}, u32[]{:S(2)}) %collective-permute-start.5) | collective-permute-done | bytes 196640 | tf_op jit(solution)/shard_map/ppermute | solution.py:300
  102.1 1.1 pad_maximum_fusion.halo
  103.2 0.0 collective-permute-done.left
  103.2 0.0 copy-start
  103.2 0.0 collective-permute-done.1.right
  103.2 0.0 copy-start.1
  103.2 1.3 copy-done
  104.5 0.5 copy-done.1
  105.0 27.2 %advect.1 = f32[6,2192,128]{2,1,0:T(8,128)} custom-call(f32[4,6,144,128]{3,2,1,0:T(8,128)} %copy-done, f32[4,6,144,128]{3,2,1,0:T(8,128)} %get-tuple-element.10.lo, f32[8,6,144,128]{3,2,1,0:T(8,128)} %get-tuple-element.13.mid, f32[4,6,144,128]{3,2,1,0:T(8,128)} %get-tuple-element.9.hi, f32[4,6,144,128]{3,2,1,0:T(8,128)} %copy-done.1, ...), custom_call_target="tpu_custom_call" | custom-call | flops 101007360 | bytes 20201472 | tf_op jit(solution)/shard_map/advect/pallas_call | solution.py:337
  (3 shorter events, 0.0 us)
Async XLA Ops:
  23.5 79.7 %collective-permute-start = (f32[4,6,144,128]{3,2,1,0:T(8,128)}, f32[4,6,144,128]{3,2,1,0:T(8,128)S(1)}, u32[]{:S(2)}, u32[]{:S(2)}) collective-permute-start(f32[4,6,144,128]{3,2,1,0:T(8,128)} %get-tuple-element.9.hi), channel_id=1, source_target_pairs={{0,1},{1,2},{2,3},{3,4},{4,5},{5,6},{6,7},{7,0},{8,9},{9,10},{10,1... | collective-permute-start | bytes 5308424 | tf_op jit(solution)/shard_map/ppermute | solution.py:299
  25.3 77.8 %collective-permute-start.1 = (f32[4,6,144,128]{3,2,1,0:T(8,128)}, f32[4,6,144,128]{3,2,1,0:T(8,128)S(1)}, u32[]{:S(2)}, u32[]{:S(2)}) collective-permute-start(f32[4,6,144,128]{3,2,1,0:T(8,128)} %get-tuple-element.10.lo), channel_id=1, source_target_pairs={{1,0},{2,1},{3,2},{4,3},{5,4},{6,5},{7,6},{0,7},{9,8},{10,9},{11,1... | collective-permute-start | bytes 5308424 | tf_op jit(solution)/shard_map/ppermute | solution.py:300
  53.2 18.9 %collective-permute-start.3 = (f32[16,6,2,8,128]{4,3,2,1,0:T(8,128)}, f32[16,6,2,8,128]{4,3,2,1,0:T(8,128)}, u32[]{:S(2)}, u32[]{:S(2)}) collective-permute-start(f32[16,6,2,8,128]{4,3,2,1,0:T(8,128)} %get-tuple-element.14.px), channel_id=1, source_target_pairs={{8,0},{16,8},{24,16},{9,1},{17,9},{25,17},{10,2},{18,10},{26,18},{... | collective-permute-start | bytes 2359304 | tf_op jit(solution)/shard_map/ppermute | solution.py:300
  56.3 33.1 %collective-permute-start.2 = (f32[16,6,2,8,128]{4,3,2,1,0:T(8,128)}, f32[16,6,2,8,128]{4,3,2,1,0:T(8,128)}, u32[]{:S(2)}, u32[]{:S(2)}) collective-permute-start(f32[16,6,2,8,128]{4,3,2,1,0:T(8,128)} %get-tuple-element.14.px), channel_id=1, source_target_pairs={{0,8},{8,16},{16,24},{1,9},{9,17},{17,25},{2,10},{10,18},{18,26},{... | collective-permute-start | bytes 2359304 | tf_op jit(solution)/shard_map/ppermute | solution.py:299
  90.9 6.6 %collective-permute-start.4 = (f32[4,6,2,8,128]{4,3,2,1,0:T(8,128)S(1)}, f32[4,6,2,8,128]{4,3,2,1,0:T(8,128)S(1)}, u32[]{:S(2)}, u32[]{:S(2)}) collective-permute-start(f32[4,6,2,8,128]{4,3,2,1,0:T(8,128)S(1)} %get-tuple-element.18), channel_id=1, source_target_pairs={{0,1},{1,2},{2,3},{3,4},{4,5},{5,6},{6,7},{7,0},{8,9},{9,10},{10,1... | collective-permute-start | bytes 589832 | tf_op jit(solution)/shard_map/ppermute | solution.py:299
  94.9 7.1 %collective-permute-start.5 = (f32[4,6,2,8,128]{4,3,2,1,0:T(8,128)S(1)}, f32[4,6,2,8,128]{4,3,2,1,0:T(8,128)S(1)}, u32[]{:S(2)}, u32[]{:S(2)}) collective-permute-start(f32[4,6,2,8,128]{4,3,2,1,0:T(8,128)S(1)} %get-tuple-element.19), channel_id=1, source_target_pairs={{1,0},{2,1},{3,2},{4,3},{5,4},{6,5},{7,6},{0,7},{9,8},{10,9},{11,1... | collective-permute-start | bytes 589832 | tf_op jit(solution)/shard_map/ppermute | solution.py:300
  103.2 1.3 copy-start
  103.2 1.8 %copy-start.1 = (f32[4,6,144,128]{3,2,1,0:T(8,128)}, f32[4,6,144,128]{3,2,1,0:T(8,128)S(1)}, u32[]{:S(2)}) copy-start(f32[4,6,144,128]{3,2,1,0:T(8,128)S(1)} %collective-permute-done.1.right) | copy-start | bytes 5308420

commit v3 on v2

--- a/solution.py
+++ b/solution.py
@@ -11,7 +11,6 @@
 ITERS = 3
 LANES = 128
 HALO = 4
-VMEM_LIMIT = 56 * 1024 * 1024
 
 
 def silu(v):
@@ -20,7 +19,7 @@
 
 
 def network(z, w_in, w_hidden, w_out, h_a, h_b, out):
-    hid = w_in.shape[0]
+    hid = w_in.shape[1]
     part = 256
 
     def layer(weight, source, target):
@@ -33,7 +32,7 @@
                 target[m - part : m, :] = silu(ready).astype(jnp.bfloat16)
             ready = acc
 
-    layer(lambda m: w_in[m : m + part, :], z, h_a)
+    layer(lambda m: w_in[:, m : m + part].T, z, h_a)
     layer(lambda m: w_hidden[0, m : m + part, :], h_a[...], h_b)
     layer(lambda m: w_hidden[1, m : m + part, :], h_b[...], h_a)
     out[: w_out.shape[0], :] = jnp.dot(w_out[...], h_a[...], preferred_element_type=jnp.float32)
@@ -111,37 +110,52 @@
 
 
 def inner_kernel(
-    levels, lon, groups, tiles, state, conv, micro, w_in, w_hidden, w_out, lo, hi, tlo, thi,
-    mid, tend, packed, h_a, h_b, out,
+    levels, lon, tiles, state, conv, micro, w_in, w_hidden, w_out, lo, hi,
+    mid, tmid, packed, q_up, q_down, h_a, h_b, out,
 ):
+    blank = jnp.zeros((mid.shape[2] - levels, LANES), jnp.float32)
+
     @pl.loop(0, (lon - 2 * HALO) // 4)
     def _(i):
         rows = [HALO + 4 * i + k for k in range(4)]
-        blank = jnp.zeros((mid.shape[2] - levels, LANES), jnp.float32)
 
         def put(k, f, upd, tnd):
             mid[4 * i + k, f, :levels, :] = upd
             mid[4 * i + k, f, levels:, :] = blank
-            tend[pl.ds(f * levels * lon + rows[k], levels, stride=lon), :] = tnd
+            tmid[4 * i + k, f, :levels, :] = tnd
 
         physics_rows(rows, levels, lon, state, conv, micro, (w_in, w_hidden, w_out), (h_a, h_b, out), put)
 
-    @pl.loop(0, HALO)
-    def _(i):
-        for f in range(6):
-            tend[pl.ds(f * levels * lon + i, levels, stride=lon), :] = tlo[i, f, :levels, :]
-            tend[pl.ds(f * levels * lon + lon - HALO + i, levels, stride=lon), :] = thi[i, f, :levels, :]
-
     lane = lax.broadcasted_iota(jnp.int32, (8, LANES), 1)
+    lower = lane % 8 < 4
     for source, first, count in ((lo, 0, HALO), (mid, HALO, lon - 2 * HALO), (hi, lon - HALO, HALO)):
 
         @pl.loop(0, count)
         def _(i, source=source, first=first):
+            done = []
             for f in range(6):
-                for g in range(groups):
-                    packed[first + i, f, g] = pack(
-                        lambda j: source[i, f, pl.ds((g * tiles + j) * 8, 8), :], tiles, lane
-                    )
+                a, b = (
+                    pack(lambda j: source[i, f, pl.ds((g * tiles + j) * 8, 8), :], tiles, lane)
+                    for g in range(2)
+                )
+                up = jnp.where(lower, a, pltpu.roll(b, 4, 1))
+                down = jnp.where(lower, pltpu.roll(b, LANES - 4, 1), a)
+                done.append((a, b, up, down))
+            for f, (a, b, up, down) in enumerate(done):
+                packed[first + i, f, 0] = a
+                packed[first + i, f, 1] = b
+                q_up[first + i, f] = up
+                q_down[first + i, f] = down
+
+
+def gather_kernel(levels, lon, tlo, tmid, thi, tend):
+    for source, first, count in ((tlo, 0, HALO), (tmid, HALO, lon - 2 * HALO), (thi, lon - HALO, HALO)):
+
+        @pl.loop(0, count)
+        def _(i, source=source, first=first):
+            got = [source[i, f, :levels, :] for f in range(6)]
+            for f in range(6):
+                tend[pl.ds(f * levels * lon + first + i, levels, stride=lon), :] = got[f]
 
 
 def split(x):
@@ -165,12 +179,14 @@
 def matrices(lat, tiles):
     lanes = np.arange(lat)
     slot, group = lanes % 8, lanes // 8
-    beyond = np.where(slot < 4, slot - 4, lat + slot - 4)
     own = np.where(slot < 4, lat + slot - 4, slot - 4)
-    center = twice(banded(lanes, lanes))
-    edges = np.stack([twice(banded(beyond, lanes) * (group == j)[:, None]) for j in range(tiles)])
     same = np.concatenate([group[:, None] == group[None, :]] * 2, axis=1)
-    return center, edges, twice(banded(beyond, beyond) * same), twice(banded(own, beyond) * same)
+    edges, packed, owned = [], [], []
+    for beyond in (np.where(slot < 4, slot - 4, lat + slot - 4), np.where(slot < 4, lat + slot, slot - 8)):
+        edges.append([twice(banded(beyond, lanes) * (group == j)[:, None]) for j in range(tiles)])
+        packed.append(twice(banded(beyond, beyond) * same))
+        owned.append(twice(banded(own, beyond) * same))
+    return twice(banded(lanes, lanes)), np.array(edges), np.array(packed), np.array(owned)
 
 
 def stencil(center, xs, y, wind_u, wind_v):
@@ -221,8 +237,8 @@
     beyond = rows_of(halo[...])
     halo_parts[...] = split(beyond)
     own = jnp.concatenate([rows_of(px_side[:2]), rows_of(px[...]), rows_of(px_side[2:])], axis=0)
-    y[...] = dot(halo_parts[2 * n : (ext - 2) * n, :], m_packed[...]) + dot(split(own), m_own[...])
-    keep = jnp.concatenate([inside[...]] * 6, axis=0)
+    y[...] = dot(halo_parts[2 * n : (ext - 2) * n, :], m_packed[0]) + dot(split(own), m_own[0])
+    keep = jnp.concatenate([inside[0]] * 6, axis=0)
     for r in range(2, ext - 2):
         c = rows_of(halo[r])
         xs = [rows_of(halo[r + d]) for d in (-2, -1, 1, 2)]
@@ -238,7 +254,7 @@
             return rows_of(ref[i, :, rows, :])
 
         cells = jnp.concatenate([at(r) for r in range(2, ext - 2)], axis=0)
-        y[...] = dot(split(cells), m_center[...]) + dot(halo_parts[2 * n : (ext - 2) * n, :], m_edges[t])
+        y[...] = dot(split(cells), m_center[...]) + dot(halo_parts[2 * n : (ext - 2) * n, :], m_edges[0, t])
         for r in range(2, ext - 2):
             c = at(r)
             xs = [at(r + d) for d in (-2, -1, 1, 2)]
@@ -246,7 +262,7 @@
             s1[k * n : (k + 1) * n, :] = stencil(c, xs, y[k * n : (k + 1) * n, :], *winds(c))
         last = lon * n
         y[:last, :] = dot(split(s1[2 * n : 2 * n + last, :]), m_center[...]) + dot(
-            s1_parts[2 * n : 2 * n + last, :], m_edges[t]
+            s1_parts[2 * n : 2 * n + last, :], m_edges[0, t]
         )
         for r in range(lon):
             c = s1[(r + 2) * n : (r + 3) * n, :]
@@ -266,7 +282,10 @@
     cells = state.reshape(flat, lat)
     f32 = jnp.float32
     full = pl.BlockSpec(memory_space=pltpu.VMEM)
-    params = pltpu.CompilerParams(vmem_limit_bytes=VMEM_LIMIT)
+
+    def limit(mib):
+        return pltpu.CompilerParams(vmem_limit_bytes=mib * 1024 * 1024)
+
     scratch = [
         pltpu.VMEM((hid, 4 * lat), jnp.bfloat16),
         pltpu.VMEM((hid, 4 * lat), jnp.bfloat16),
@@ -287,10 +306,10 @@
         in_specs=[full] * 6,
         out_specs=[full] * 4,
         scratch_shapes=scratch,
-        compiler_params=params,
+        compiler_params=limit(32),
         cost_estimate=cost(2 * HALO),
         name="physics_edge",
-    )(cells, conv_mask, micro_mask, w_in, w_hidden, w_out)
+    )(cells, conv_mask, micro_mask, w_in.T, w_hidden, w_out)
 
     def both(axis, up, down, closed):
         n = lax.axis_size(axis)
@@ -301,29 +320,43 @@
         )
 
     left, right = both("col", hi, lo, True)
-    mid, tend, px = pl.pallas_call(
-        functools.partial(inner_kernel, levels, lon, groups, tiles),
+    row_shape = jax.ShapeDtypeStruct((lon - 2 * HALO, fields, pad, lat), f32)
+    q_shape = jax.ShapeDtypeStruct((lon, fields, 8, lat), f32)
+    mid, tmid, px, q_up, q_down = pl.pallas_call(
+        functools.partial(inner_kernel, levels, lon, tiles),
         out_shape=[
-            jax.ShapeDtypeStruct((lon - 2 * HALO, fields, pad, lat), f32),
-            jax.ShapeDtypeStruct((flat, lat), f32),
+            row_shape,
+            row_shape,
             jax.ShapeDtypeStruct((lon, fields, groups, 8, lat), f32),
+            q_shape,
+            q_shape,
         ],
-        in_specs=[full] * 10,
-        out_specs=[full] * 3,
+        in_specs=[full] * 8,
+        out_specs=[full] * 5,
         scratch_shapes=scratch,
-        compiler_params=params,
+        compiler_params=limit(36),
         cost_estimate=cost(lon - 2 * HALO),
         name="physics_inner",
-    )(cells, conv_mask, micro_mask, w_in, w_hidden, w_out, lo, hi, tlo, thi)
-
-    before, after = both("row", px, px, False)
-    slot = lax.broadcasted_iota(jnp.int32, (8, lat), 1) % 8
-    own = jnp.where(slot < 4, before, after)
+    )(cells, conv_mask, micro_mask, w_in.T, w_hidden, w_out, lo, hi)
+
+    before, after = both("row", q_up, q_down, False)
+    tend = pl.pallas_call(
+        functools.partial(gather_kernel, levels, lon),
+        out_shape=jax.ShapeDtypeStruct((flat, lat), f32),
+        in_specs=[full] * 3,
+        out_specs=full,
+        compiler_params=limit(20),
+        cost_estimate=pl.CostEstimate(flops=flat * lat, bytes_accessed=8 * flat * lat, transcendentals=0),
+        name="gather_tendency",
+    )(tlo, tmid, thi)
+    lower = lax.broadcasted_iota(jnp.int32, (8, lat), 1) % 8 < 4
+    own = jnp.stack([jnp.where(lower, before, after), jnp.where(lower, after, before)], axis=2)
     corner_l, corner_r = both("col", own[lon - HALO :], own[:HALO], True)
     halo = jnp.concatenate([corner_l, own, corner_r], axis=0)
     row = lax.axis_index("row")
     first, last = row == 0, row == lax.axis_size("row") - 1
-    inside = jnp.where(jnp.where(slot < 4, first, last), 0.0, 1.0).astype(f32)
+    outside = jnp.stack([jnp.where(lower, first, last), jnp.where(lower, last, first)])
+    inside = jnp.where(outside, 0.0, 1.0).astype(f32)
 
     ext = lon + 2 * HALO
     center, edges, packed, own_edges = (jnp.asarray(m) for m in matrices(lat, tiles))
@@ -346,11 +379,11 @@
             rows_spec(HALO),
             packed_spec(lon),
             packed_spec(ext),
-            pl.BlockSpec((8, lat), lambda g: (0, 0)),
+            pl.BlockSpec((1, 8, lat), lambda g: (g, 0, 0)),
             pl.BlockSpec(center.shape, lambda g: (0, 0)),
-            pl.BlockSpec(edges.shape, lambda g: (0, 0, 0)),
-            pl.BlockSpec(packed.shape, lambda g: (0, 0)),
-            pl.BlockSpec(own_edges.shape, lambda g: (0, 0)),
+            pl.BlockSpec((1,) + edges.shape[1:], lambda g: (g, 0, 0, 0)),
+            pl.BlockSpec((1,) + packed.shape[1:], lambda g: (g, 0, 0)),
+            pl.BlockSpec((1,) + own_edges.shape[1:], lambda g: (g, 0, 0)),
         ],
         out_specs=pl.BlockSpec((fields, 8 * tiles * lon, lat), lambda g: (0, g, 0)),
         scratch_shapes=[
@@ -360,7 +393,7 @@
             pltpu.VMEM(((ext - 4) * 48, 2 * lat), f32),
             pltpu.VMEM(((ext - 4) * 48, lat), f32),
         ],
-        compiler_params=params,
+        compiler_params=limit(36),
         cost_estimate=pl.CostEstimate(
             flops=60 * flat * lat, bytes_accessed=12 * flat * lat, transcendentals=0
         ),

time: 132 us -> 117 us (0.89)
  the two profiles are of different devices: /device:TPU:5 before, /device:TPU:0 now
where the time goes in v3:
time: 117 us; the launch traced here: 116 us
  Pallas kernels  67.3 us (58%)
  local copies, waits for them, and re-layouts  17.3 us (15%)
  waiting for transfers between devices  15.3 us (13%)
  starting transfers between devices  14 us (12%)
  other arithmetic  1.31 us (1%)
    pallas_call x1, Pallas kernels, local(): pl.pallas_call(functools.partial(advect_kernel, lon, tiles), grid=(groups...  26.1 us
    pallas_call x1, Pallas kernels, local(): pl.pallas_call(functools.partial(inner_kernel, levels, lon, tiles), out_s...  21.7 us
    unnamed x40, local copies, waits for them, and re-layouts  17.3 us
    pallas_call x1, Pallas kernels, local(): pl.pallas_call(functools.partial(edge_kernel, levels, lon), out_shape=[ed...  13.1 us
    ppermute x3, waiting for transfers between devices, both(): lax.ppermute(down, axis, [((i + 1) % n, i) for i in range(ends)])  10.4 us
    ppermute x3, starting transfers between devices, both(): lax.ppermute(down, axis, [((i + 1) % n, i) for i in range(ends)])  8.85 us
    pallas_call x1, Pallas kernels, local(): pl.pallas_call(functools.partial(gather_kernel, levels, lon), out_shape=j...  6.43 us
    ppermute x3, starting transfers between devices, both(): lax.ppermute(up, axis, [(i, (i + 1) % n) for i in range(ends)])  5.19 us
  transfers between devices with their start and end apart: 6, of which 2 were waited for; matrix products, arithmetic and copies ran while one was open for 1% of the time, Pallas kernels for 24%

profile of v3, /device:TPU:0, one launch (start us, length us, event | category | flops | bytes accessed | tf_op | source)
XLA Modules:
  0.0 116.1 jit_solution(9838433024937825153)
XLA Ops:
  0.6 0.0 copy-start.12
  0.6 2.9 %copy-done.12 = f32[6,137,16,128]{3,2,1,0:T(8,128)S(1)} copy-done((f32[6,137,16,128]{3,2,1,0:T(8,128)S(1)}, f32[6,137,16,128]{3,2,1,0:T(8,128)}, u32[]{:S(2)}) %copy-start.12) | copy-done | bytes 6733848
  3.5 0.0 copy-start.13
  3.5 2.2 %copy-done.13 = bf16[2,1024,1024]{2,1,0:T(8,128)(2,1)S(1)} copy-done((bf16[2,1024,1024]{2,1,0:T(8,128)(2,1)S(1)}, bf16[2,1024,1024]{2,1,0:T(8,128)(2,1)}, u32[]{:S(2)}) %copy-start.13) | copy-done | bytes 4194328
  5.7 0.0 copy-start.14
  5.7 1.4 %copy-done.14 = bf16[1024,822]{0,1:T(8,128)(2,1)S(1)} copy-done((bf16[1024,822]{0,1:T(8,128)(2,1)S(1)}, bf16[1024,822]{0,1:T(8,128)(2,1)}, u32[]{:S(2)}) %copy-start.14) | copy-done | bytes 1683480
  7.2 0.0 copy-start.16
  7.2 1.3 %copy-done.16 = bf16[548,1024]{1,0:T(8,128)(2,1)S(1)} copy-done((bf16[548,1024]{1,0:T(8,128)(2,1)S(1)}, bf16[548,1024]{1,0:T(8,128)(2,1)}, u32[]{:S(2)}) %copy-start.16) | copy-done | bytes 1122328
  8.4 0.0 copy-start.18
  8.4 0.7 copy-done.18
  9.1 0.0 copy-start.19
  9.1 0.7 copy-done.19
  9.8 0.0 copy-start.15
  9.8 0.0 copy-start.17
  9.8 13.1 %physics_edge.1 = (f32[4,6,144,128]{3,2,1,0:T(8,128)}, f32[4,6,144,128]{3,2,1,0:T(8,128)}, f32[4,6,144,128]{3,2,1,0:T(8,128)S(1)}, f32[4,6,144,128]{3,2,1,0:T(8,128)S(1)}) custom-call(f32[13152,128]{1,0:T(8,128)S(1)} %bitcast.11, s32[16,128]{1,0:T(8,128)S(1)} %copy-done.18, s32[16,128]{1,0:T(8,128)S(1)} %copy-done.19, bf16[822,1024]{1,0:T(8,128)(2,1)S(1)} %bitcast.12, ...), custom_call_target="tpu_custom_call" | custom-call | flops 7168065536 | bytes 20467712 | tf_op jit(solution)/shard_map/physics_edge/pallas_call | solution.py:303
  22.9 0.0 copy-start.3
  22.9 1.2 %copy-done.3 = f32[4,6,144,128]{3,2,1,0:T(8,128)} copy-done((f32[4,6,144,128]{3,2,1,0:T(8,128)}, f32[4,6,144,128]{3,2,1,0:T(8,128)S(1)}, u32[]{:S(2)}) %copy-start.3) | copy-done | bytes 1769496
  24.1 0.0 copy-start.5
  24.1 1.3 %copy-done.5 = f32[4,6,144,128]{3,2,1,0:T(8,128)} copy-done((f32[4,6,144,128]{3,2,1,0:T(8,128)}, f32[4,6,144,128]{3,2,1,0:T(8,128)S(1)}, u32[]{:S(2)}) %copy-start.5) | copy-done | bytes 1769496
  25.4 0.5 collective-permute-start
  25.8 4.0 %collective-permute-start.1 = (f32[4,6,144,128]{3,2,1,0:T(8,128)}, f32[4,6,144,128]{3,2,1,0:T(8,128)}, u32[]{:S(2)}, u32[]{:S(2)}) collective-permute-start(f32[4,6,144,128]{3,2,1,0:T(8,128)} %get-tuple-element.12.lo), channel_id=1, source_target_pairs={{1,0},{2,1},{3,2},{4,3},{5,4},{6,5},{7,6},{0,7},{9,8},{10,9},{11,1... | collective-permute-start | bytes 5308424 | tf_op jit(solution)/shard_map/ppermute | solution.py:319
  29.9 0.0 copy-done.15
  29.9 0.0 copy-done.17
  29.9 21.7 %physics_inner.1 = (f32[8,6,144,128]{3,2,1,0:T(8,128)S(1)}, f32[8,6,144,128]{3,2,1,0:T(8,128)S(1)}, f32[16,6,2,8,128]{4,3,2,1,0:T(8,128)S(1)}, f32[16,6,8,128]{3,2,1,0:T(8,128)}, f32[16,6,8,128]{3,2,1,0:T(8,128)}) custom-call(f32[13152,128]{1,0:T(8,128)} %bitcast.10, s32[16,128]{1,0:T(8,128)S(1)} %copy-done.18, s32[16,128]{1,0:T(8,128)S(1)} %copy-done.19, ...), custom_call_target="tpu_custom_call" | custom-call | flops 7168065536 | bytes 20467712 | tf_op jit(solution)/shard_map/physics_inner/pallas_call | solution.py:325
  51.5 0.0 copy-start
  51.5 1.8 %copy-done = f32[8,6,144,128]{3,2,1,0:T(8,128)} copy-done((f32[8,6,144,128]{3,2,1,0:T(8,128)}, f32[8,6,144,128]{3,2,1,0:T(8,128)S(1)}, u32[]{:S(2)}) %copy-start) | copy-done | bytes 3538968
  53.3 0.0 copy-start.7
  53.3 0.9 copy-done.7
  54.2 4.7 %collective-permute-start.2 = (f32[16,6,8,128]{3,2,1,0:T(8,128)}, f32[16,6,8,128]{3,2,1,0:T(8,128)}, u32[]{:S(2)}, u32[]{:S(2)}) collective-permute-start(f32[16,6,8,128]{3,2,1,0:T(8,128)} %get-tuple-element.15), channel_id=1, source_target_pairs={{0,8},{8,16},{16,24},{1,9},{9,17},{17,25},{2,10},{10,18},{18,26},{... | collective-permute-start | bytes 1179656 | tf_op jit(solution)/shard_map/ppermute | solution.py:318
  58.9 1.3 %collective-permute-start.3 = (f32[16,6,8,128]{3,2,1,0:T(8,128)}, f32[16,6,8,128]{3,2,1,0:T(8,128)}, u32[]{:S(2)}, u32[]{:S(2)}) collective-permute-start(f32[16,6,8,128]{3,2,1,0:T(8,128)} %get-tuple-element.16), channel_id=1, source_target_pairs={{8,0},{16,8},{24,16},{9,1},{17,9},{25,17},{10,2},{18,10},{26,18},{... | collective-permute-start | bytes 1179656 | tf_op jit(solution)/shard_map/ppermute | solution.py:319
  60.2 0.0 copy-start.4
  60.2 4.9 %collective-permute-done.2 = f32[16,6,8,128]{3,2,1,0:T(8,128)} collective-permute-done((f32[16,6,8,128]{3,2,1,0:T(8,128)}, f32[16,6,8,128]{3,2,1,0:T(8,128)}, u32[]{:S(2)}, u32[]{:S(2)}) %collective-permute-start.2) | collective-permute-done | bytes 393248 | tf_op jit(solution)/shard_map/ppermute | solution.py:318
  65.1 10.4 %collective-permute-done.3 = f32[16,6,8,128]{3,2,1,0:T(8,128)} collective-permute-done((f32[16,6,8,128]{3,2,1,0:T(8,128)}, f32[16,6,8,128]{3,2,1,0:T(8,128)}, u32[]{:S(2)}, u32[]{:S(2)}) %collective-permute-start.3) | collective-permute-done | bytes 393248 | tf_op jit(solution)/shard_map/ppermute | solution.py:319
  75.5 1.2 %select_bitcast_fusion.1 = (f32[16,6,1,8,128]{4,3,2,1,0:T(8,128)S(1)}, f32[16,6,1,8,128]{4,3,2,1,0:T(8,128)S(1)}) fusion(f32[16,6,8,128]{3,2,1,0:T(8,128)} %collective-permute-done.2, f32[16,6,8,128]{3,2,1,0:T(8,128)} %collective-permute-done.3, pred[8,128]{1,0:T(8,128)(4,1)S(1)} %select_compare_fusion.1), kind=kLoop, calls=%fused_computation.2 | loop fusion | flops 196608 | bytes 1573888 | tf_op jit(solution)/shard_map/stack | solution.py:353
  76.7 0.1 collective-permute-start.4
  76.8 3.5 %collective-permute-start.5 = (f32[4,6,2,8,128]{4,3,2,1,0:T(8,128)S(1)}, f32[4,6,2,8,128]{4,3,2,1,0:T(8,128)S(1)}, u32[]{:S(2)}, u32[]{:S(2)}) collective-permute-start(f32[4,6,2,8,128]{4,3,2,1,0:T(8,128)S(1)} %get-tuple-element.23), channel_id=1, source_target_pairs={{1,0},{2,1},{3,2},{4,3},{5,4},{6,5},{7,6},{0,7},{9,8},{10,9},{11,1... | collective-permute-start | bytes 589832 | tf_op jit(solution)/shard_map/ppermute | solution.py:319
  80.3 0.0 copy-done.4
  80.3 0.0 copy-start.6
  80.3 1.5 %copy-done.6 = f32[4,6,144,128]{3,2,1,0:T(8,128)S(1)} copy-done((f32[4,6,144,128]{3,2,1,0:T(8,128)S(1)}, f32[4,6,144,128]{3,2,1,0:T(8,128)}, u32[]{:S(2)}) %copy-start.6) | copy-done | bytes 1769496
  81.8 0.0 copy-start.1
  81.8 0.0 copy-start.8
  81.8 0.0 copy-start.9
  81.8 0.0 copy-start.10
  81.8 0.0 copy-start.11
  81.8 6.4 %gather_tendency.1 = f32[13152,128]{1,0:T(8,128)} custom-call(f32[4,6,144,128]{3,2,1,0:T(8,128)S(1)} %copy-done.4, f32[8,6,144,128]{3,2,1,0:T(8,128)S(1)} %get-tuple-element.18.tmid, f32[4,6,144,128]{3,2,1,0:T(8,128)S(1)} %copy-done.6), custom_call_target="tpu_custom_call" | custom-call | flops 1683456 | bytes 13467648 | tf_op jit(solution)/shard_map/gather_tendency/pallas_call | solution.py:343
  88.2 0.0 copy-start.2
  88.3 0.0 collective-permute-done.4
  88.3 0.0 collective-permute-done.5
  88.3 0.1 pad_maximum_fusion.halo
  88.4 0.0 collective-permute-done.left
  88.4 0.0 collective-permute-done.1.right
  88.4 0.0 copy-done.1
  88.4 0.0 copy-done.8
  88.4 0.0 copy-done.9
  88.4 0.0 copy-done.10
  88.4 0.0 copy-done.11
  88.4 1.5 %copy-done.2 = bf16[2,9,256,256]{3,2,1,0:T(8,128)(2,1)S(1)} copy-done((bf16[2,9,256,256]{3,2,1,0:T(8,128)(2,1)S(1)}, bf16[2,9,256,256]{3,2,1,0:T(8,128)(2,1)}, u32[]{:S(2)}) %copy-start.2) | copy-done | bytes 2359320
  89.9 26.1 %advect.1 = f32[6,2192,128]{2,1,0:T(8,128)} custom-call(f32[4,6,144,128]{3,2,1,0:T(8,128)} %collective-permute-done.left, f32[4,6,144,128]{3,2,1,0:T(8,128)} %get-tuple-element.12.lo, f32[8,6,144,128]{3,2,1,0:T(8,128)S(1)} %copy-done.1, f32[4,6,144,128]{3,2,1,0:T(8,128)} %get-tuple-element.11.hi, f32[4,6,144,128]{3,2,1,0:T(8,128)} %collective-permute-done.1.right, ...), custom_call_target="tpu_custom_call" | custom-call | flops 101007360 | bytes 20201472 | tf_op jit(solution)/shard_map/advect/pallas_call | solution.py:370
  (6 shorter events, 0.1 us)
Async XLA Ops:
  0.6 2.9 %copy-start.12 = (f32[6,137,16,128]{3,2,1,0:T(8,128)S(1)}, f32[6,137,16,128]{3,2,1,0:T(8,128)}, u32[]{:S(2)}) copy-start(f32[6,137,16,128]{3,2,1,0:T(8,128)} %param.10) | copy-start | bytes 20201476
  3.5 2.2 %copy-start.13 = (bf16[2,1024,1024]{2,1,0:T(8,128)(2,1)S(1)}, bf16[2,1024,1024]{2,1,0:T(8,128)(2,1)}, u32[]{:S(2)}) copy-start(bf16[2,1024,1024]{2,1,0:T(8,128)(2,1)} %w_hidden.3) | copy-start | bytes 12582916
  5.7 1.4 %copy-start.14 = (bf16[1024,822]{0,1:T(8,128)(2,1)S(1)}, bf16[1024,822]{0,1:T(8,128)(2,1)}, u32[]{:S(2)}) copy-start(bf16[1024,822]{0,1:T(8,128)(2,1)} %param.13) | copy-start | bytes 5050372
  7.2 1.3 %copy-start.16 = (bf16[548,1024]{1,0:T(8,128)(2,1)S(1)}, bf16[548,1024]{1,0:T(8,128)(2,1)}, u32[]{:S(2)}) copy-start(bf16[548,1024]{1,0:T(8,128)(2,1)} %w_out.3) | copy-start | bytes 3366916
  8.4 0.7 copy-start.18
  9.1 0.7 copy-start.19
  9.8 20.0 %copy-start.15 = (bf16[1024,822]{0,1:T(8,128)(2,1)S(1)}, bf16[1024,822]{0,1:T(8,128)(2,1)}, u32[]{:S(2)}) copy-start(bf16[1024,822]{0,1:T(8,128)(2,1)} %param.13) | copy-start | bytes 5050372
  9.8 20.1 %copy-start.17 = (bf16[548,1024]{1,0:T(8,128)(2,1)S(1)}, bf16[548,1024]{1,0:T(8,128)(2,1)}, u32[]{:S(2)}) copy-start(bf16[548,1024]{1,0:T(8,128)(2,1)} %w_out.3) | copy-start | bytes 3366916
  22.9 1.2 %copy-start.3 = (f32[4,6,144,128]{3,2,1,0:T(8,128)}, f32[4,6,144,128]{3,2,1,0:T(8,128)S(1)}, u32[]{:S(2)}) copy-start(f32[4,6,144,128]{3,2,1,0:T(8,128)S(1)} %get-tuple-element.17.tlo) | copy-start | bytes 5308420
  24.1 1.3 %copy-start.5 = (f32[4,6,144,128]{3,2,1,0:T(8,128)}, f32[4,6,144,128]{3,2,1,0:T(8,128)S(1)}, u32[]{:S(2)}) copy-start(f32[4,6,144,128]{3,2,1,0:T(8,128)S(1)} %get-tuple-element.19.thi) | copy-start | bytes 5308420
  25.4 63.0 %collective-permute-start = (f32[4,6,144,128]{3,2,1,0:T(8,128)}, f32[4,6,144,128]{3,2,1,0:T(8,128)}, u32[]{:S(2)}, u32[]{:S(2)}) collective-permute-start(f32[4,6,144,128]{3,2,1,0:T(8,128)} %get-tuple-element.11.hi), channel_id=1, source_target_pairs={{0,1},{1,2},{2,3},{3,4},{4,5},{5,6},{6,7},{7,0},{8,9},{9,10},{10,1... | collective-permute-start | bytes 5308424 | tf_op jit(solution)/shard_map/ppermute | solution.py:318
  25.8 62.5 %collective-permute-start.1 = (f32[4,6,144,128]{3,2,1,0:T(8,128)}, f32[4,6,144,128]{3,2,1,0:T(8,128)}, u32[]{:S(2)}, u32[]{:S(2)}) collective-permute-start(f32[4,6,144,128]{3,2,1,0:T(8,128)} %get-tuple-element.12.lo), channel_id=1, source_target_pairs={{1,0},{2,1},{3,2},{4,3},{5,4},{6,5},{7,6},{0,7},{9,8},{10,9},{11,1... | collective-permute-start | bytes 5308424 | tf_op jit(solution)/shard_map/ppermute | solution.py:319
  51.5 1.8 %copy-start = (f32[8,6,144,128]{3,2,1,0:T(8,128)}, f32[8,6,144,128]{3,2,1,0:T(8,128)S(1)}, u32[]{:S(2)}) copy-start(f32[8,6,144,128]{3,2,1,0:T(8,128)S(1)} %get-tuple-element.13.mid) | copy-start | bytes 10616836
  53.3 0.9 copy-start.7
  54.2 10.9 %collective-permute-start.2 = (f32[16,6,8,128]{3,2,1,0:T(8,128)}, f32[16,6,8,128]{3,2,1,0:T(8,128)}, u32[]{:S(2)}, u32[]{:S(2)}) collective-permute-start(f32[16,6,8,128]{3,2,1,0:T(8,128)} %get-tuple-element.15), channel_id=1, source_target_pairs={{0,8},{8,16},{16,24},{1,9},{9,17},{17,25},{2,10},{10,18},{18,26},{... | collective-permute-start | bytes 1179656 | tf_op jit(solution)/shard_map/ppermute | solution.py:318
  58.9 16.6 %collective-permute-start.3 = (f32[16,6,8,128]{3,2,1,0:T(8,128)}, f32[16,6,8,128]{3,2,1,0:T(8,128)}, u32[]{:S(2)}, u32[]{:S(2)}) collective-permute-start(f32[16,6,8,128]{3,2,1,0:T(8,128)} %get-tuple-element.16), channel_id=1, source_target_pairs={{8,0},{16,8},{24,16},{9,1},{17,9},{25,17},{10,2},{18,10},{26,18},{... | collective-permute-start | bytes 1179656 | tf_op jit(solution)/shard_map/ppermute | solution.py:319
  60.2 20.1 %copy-start.4 = (f32[4,6,144,128]{3,2,1,0:T(8,128)S(1)}, f32[4,6,144,128]{3,2,1,0:T(8,128)}, u32[]{:S(2)}) copy-start(f32[4,6,144,128]{3,2,1,0:T(8,128)} %copy-done.3) | copy-start | bytes 5308420
  76.7 11.5 %collective-permute-start.4 = (f32[4,6,2,8,128]{4,3,2,1,0:T(8,128)S(1)}, f32[4,6,2,8,128]{4,3,2,1,0:T(8,128)S(1)}, u32[]{:S(2)}, u32[]{:S(2)}) collective-permute-start(f32[4,6,2,8,128]{4,3,2,1,0:T(8,128)S(1)} %get-tuple-element.22), channel_id=1, source_target_pairs={{0,1},{1,2},{2,3},{3,4},{4,5},{5,6},{6,7},{7,0},{8,9},{9,10},{10,1... | collective-permute-start | bytes 589832 | tf_op jit(solution)/shard_map/ppermute | solution.py:318
  76.8 11.5 %collective-permute-start.5 = (f32[4,6,2,8,128]{4,3,2,1,0:T(8,128)S(1)}, f32[4,6,2,8,128]{4,3,2,1,0:T(8,128)S(1)}, u32[]{:S(2)}, u32[]{:S(2)}) collective-permute-start(f32[4,6,2,8,128]{4,3,2,1,0:T(8,128)S(1)} %get-tuple-element.23), channel_id=1, source_target_pairs={{1,0},{2,1},{3,2},{4,3},{5,4},{6,5},{7,6},{0,7},{9,8},{10,9},{11,1... | collective-permute-start | bytes 589832 | tf_op jit(solution)/shard_map/ppermute | solution.py:319
  80.3 1.5 %copy-start.6 = (f32[4,6,144,128]{3,2,1,0:T(8,128)S(1)}, f32[4,6,144,128]{3,2,1,0:T(8,128)}, u32[]{:S(2)}) copy-start(f32[4,6,144,128]{3,2,1,0:T(8,128)} %copy-done.5) | copy-start | bytes 5308420
  81.8 6.6 %copy-start.1 = (f32[8,6,144,128]{3,2,1,0:T(8,128)S(1)}, f32[8,6,144,128]{3,2,1,0:T(8,128)}, u32[]{:S(2)}) copy-start(f32[8,6,144,128]{3,2,1,0:T(8,128)} %copy-done) | copy-start | bytes 10616836
  81.8 6.6 %copy-start.8 = (f32[16,6,2,8,128]{4,3,2,1,0:T(8,128)S(1)}, f32[16,6,2,8,128]{4,3,2,1,0:T(8,128)}, u32[]{:S(2)}) copy-start(f32[16,6,2,8,128]{4,3,2,1,0:T(8,128)} %copy-done.7) | copy-start | bytes 2359300
  81.8 6.6 %copy-start.9 = (bf16[2,256,256]{2,1,0:T(8,128)(2,1)S(1)}, bf16[2,256,256]{2,1,0:T(8,128)(2,1)}, u32[]{:S(2)}) copy-start(bf16[2,256,256]{2,1,0:T(8,128)(2,1)} %constant.41.clone.m_own) | copy-start | bytes 786436
  81.8 6.6 %copy-start.10 = (bf16[2,256,256]{2,1,0:T(8,128)(2,1)S(1)}, bf16[2,256,256]{2,1,0:T(8,128)(2,1)}, u32[]{:S(2)}) copy-start(bf16[2,256,256]{2,1,0:T(8,128)(2,1)} %constant.40.clone.m_packed) | copy-start | bytes 786436
  81.8 6.6 %copy-start.11 = (bf16[256,256]{1,0:T(8,128)(2,1)S(1)}, bf16[256,256]{1,0:T(8,128)(2,1)}, u32[]{:S(2)}) copy-start(bf16[256,256]{1,0:T(8,128)(2,1)} %constant.38.clone.m_center) | copy-start | bytes 393220
  88.2 1.7 %copy-start.2 = (bf16[2,9,256,256]{3,2,1,0:T(8,128)(2,1)S(1)}, bf16[2,9,256,256]{3,2,1,0:T(8,128)(2,1)}, u32[]{:S(2)}) copy-start(bf16[2,9,256,256]{3,2,1,0:T(8,128)(2,1)} %constant.39.clone.m_edges) | copy-start | bytes 7077892

commit v4 on v3

--- a/solution.py
+++ b/solution.py
@@ -110,7 +110,7 @@
 
 
 def inner_kernel(
-    levels, lon, tiles, state, conv, micro, w_in, w_hidden, w_out, lo, hi,
+    levels, lon, tiles, state, conv, micro, w_in, w_hidden, w_out, _edges,
     mid, tmid, packed, q_up, q_down, h_a, h_b, out,
 ):
     blank = jnp.zeros((mid.shape[2] - levels, LANES), jnp.float32)
@@ -126,26 +126,34 @@
 
         physics_rows(rows, levels, lon, state, conv, micro, (w_in, w_hidden, w_out), (h_a, h_b, out), put)
 
+    pack_rows(mid, 0, lon - 2 * HALO, tiles, packed, q_up, q_down)
+
+
+def pack_rows(source, first, count, tiles, packed, q_up, q_down):
     lane = lax.broadcasted_iota(jnp.int32, (8, LANES), 1)
     lower = lane % 8 < 4
-    for source, first, count in ((lo, 0, HALO), (mid, HALO, lon - 2 * HALO), (hi, lon - HALO, HALO)):
-
-        @pl.loop(0, count)
-        def _(i, source=source, first=first):
-            done = []
-            for f in range(6):
-                a, b = (
-                    pack(lambda j: source[i, f, pl.ds((g * tiles + j) * 8, 8), :], tiles, lane)
-                    for g in range(2)
-                )
-                up = jnp.where(lower, a, pltpu.roll(b, 4, 1))
-                down = jnp.where(lower, pltpu.roll(b, LANES - 4, 1), a)
-                done.append((a, b, up, down))
-            for f, (a, b, up, down) in enumerate(done):
-                packed[first + i, f, 0] = a
-                packed[first + i, f, 1] = b
-                q_up[first + i, f] = up
-                q_down[first + i, f] = down
+
+    @pl.loop(0, count)
+    def _(i):
+        done = []
+        for f in range(6):
+            a, b = (
+                pack(lambda j: source[i, f, pl.ds((g * tiles + j) * 8, 8), :], tiles, lane)
+                for g in range(2)
+            )
+            up = jnp.where(lower, a, pltpu.roll(b, 4, 1))
+            down = jnp.where(lower, pltpu.roll(b, LANES - 4, 1), a)
+            done.append((a, b, up, down))
+        for f, (a, b, up, down) in enumerate(done):
+            packed[first + i, f, 0] = a
+            packed[first + i, f, 1] = b
+            q_up[first + i, f] = up
+            q_down[first + i, f] = down
+
+
+def pack_kernel(tiles, lo, hi, packed, q_up, q_down):
+    pack_rows(lo, 0, HALO, tiles, packed, q_up, q_down)
+    pack_rows(hi, HALO, HALO, tiles, packed, q_up, q_down)
 
 
 def gather_kernel(levels, lon, tlo, tmid, thi, tend):
@@ -207,7 +215,7 @@
 
 
 def advect_kernel(
-    lon, tiles, left, lo, mid, hi, right, px, halo, inside, m_center, m_edges, m_packed, m_own, adv,
+    lon, tiles, left, lo, mid, hi, right, px_edge, px_mid, halo, inside, m_center, m_edges, m_packed, m_own, adv,
     px_side, halo_parts, s1_parts, y, s1,
 ):
     lane = lax.broadcasted_iota(jnp.int32, (8, LANES), 1)
@@ -236,7 +244,8 @@
 
     beyond = rows_of(halo[...])
     halo_parts[...] = split(beyond)
-    own = jnp.concatenate([rows_of(px_side[:2]), rows_of(px[...]), rows_of(px_side[2:])], axis=0)
+    own = jnp.concatenate([rows_of(px_side[:2]), rows_of(px_edge[:HALO]), rows_of(px_mid[...]),
+         rows_of(px_edge[HALO:]), rows_of(px_side[2:])], axis=0)
     y[...] = dot(halo_parts[2 * n : (ext - 2) * n, :], m_packed[0]) + dot(split(own), m_own[0])
     keep = jnp.concatenate([inside[0]] * 6, axis=0)
     for r in range(2, ext - 2):
@@ -306,7 +315,7 @@
         in_specs=[full] * 6,
         out_specs=[full] * 4,
         scratch_shapes=scratch,
-        compiler_params=limit(32),
+        compiler_params=limit(56),
         cost_estimate=cost(2 * HALO),
         name="physics_edge",
     )(cells, conv_mask, micro_mask, w_in.T, w_hidden, w_out)
@@ -320,24 +329,34 @@
         )
 
     left, right = both("col", hi, lo, True)
+    def packed_shapes(n):
+        q = jax.ShapeDtypeStruct((n, fields, 8, lat), f32)
+        return [jax.ShapeDtypeStruct((n, fields, groups, 8, lat), f32), q, q]
+
+    px_edge, qe_up, qe_down = pl.pallas_call(
+        functools.partial(pack_kernel, tiles),
+        out_shape=packed_shapes(2 * HALO),
+        in_specs=[full] * 2,
+        out_specs=[full] * 3,
+        compiler_params=limit(20),
+        name="pack_edges",
+    )(lo, hi)
+    before_e, after_e = both("row", qe_up, qe_down, False)
     row_shape = jax.ShapeDtypeStruct((lon - 2 * HALO, fields, pad, lat), f32)
-    q_shape = jax.ShapeDtypeStruct((lon, fields, 8, lat), f32)
-    mid, tmid, px, q_up, q_down = pl.pallas_call(
+    mid, tmid, px_mid, q_up, q_down = pl.pallas_call(
         functools.partial(inner_kernel, levels, lon, tiles),
         out_shape=[
             row_shape,
             row_shape,
-            jax.ShapeDtypeStruct((lon, fields, groups, 8, lat), f32),
-            q_shape,
-            q_shape,
+            *packed_shapes(lon - 2 * HALO),
         ],
-        in_specs=[full] * 8,
+        in_specs=[full] * 6 + [pl.BlockSpec(memory_space=pl.ANY)],
         out_specs=[full] * 5,
         scratch_shapes=scratch,
-        compiler_params=limit(36),
+        compiler_params=limit(56),
         cost_estimate=cost(lon - 2 * HALO),
         name="physics_inner",
-    )(cells, conv_mask, micro_mask, w_in.T, w_hidden, w_out, lo, hi)
+    )(cells, conv_mask, micro_mask, w_in.T, w_hidden, w_out, px_edge)
 
     before, after = both("row", q_up, q_down, False)
     tend = pl.pallas_call(
@@ -350,9 +369,13 @@
         name="gather_tendency",
     )(tlo, tmid, thi)
     lower = lax.broadcasted_iota(jnp.int32, (8, lat), 1) % 8 < 4
-    own = jnp.stack([jnp.where(lower, before, after), jnp.where(lower, after, before)], axis=2)
-    corner_l, corner_r = both("col", own[lon - HALO :], own[:HALO], True)
-    halo = jnp.concatenate([corner_l, own, corner_r], axis=0)
+
+    def joined(before, after):
+        return jnp.stack([jnp.where(lower, before, after), jnp.where(lower, after, before)], axis=2)
+
+    own_e = joined(before_e, after_e)
+    corner_l, corner_r = both("col", own_e[HALO:], own_e[:HALO], True)
+    halo = jnp.concatenate([corner_l, own_e[:HALO], joined(before, after), own_e[HALO:], corner_r], axis=0)
     row = lax.axis_index("row")
     first, last = row == 0, row == lax.axis_size("row") - 1
     outside = jnp.stack([jnp.where(lower, first, last), jnp.where(lower, last, first)])
@@ -377,7 +400,8 @@
             rows_spec(lon - 2 * HALO),
             rows_spec(HALO),
             rows_spec(HALO),
-            packed_spec(lon),
+            packed_spec(2 * HALO),
+            packed_spec(lon - 2 * HALO),
             packed_spec(ext),
             pl.BlockSpec((1, 8, lat), lambda g: (g, 0, 0)),
             pl.BlockSpec(center.shape, lambda g: (0, 0)),
@@ -393,12 +417,12 @@
             pltpu.VMEM(((ext - 4) * 48, 2 * lat), f32),
             pltpu.VMEM(((ext - 4) * 48, lat), f32),
         ],
-        compiler_params=limit(36),
+        compiler_params=limit(56),
         cost_estimate=pl.CostEstimate(
             flops=60 * flat * lat, bytes_accessed=12 * flat * lat, transcendentals=0
         ),
         name="advect",
-    )(left, lo, mid, hi, right, px, halo, inside, center, edges, packed, own_edges)
+    )(left, lo, mid, hi, right, px_edge, px_mid, halo, inside, center, edges, packed, own_edges)
     return adv.reshape(state.shape), tend.reshape(state.shape)
 
 

time: 117 us -> 118 us (level)
  local copies, waits for them, and re-layouts: 17.3 us -> 6.78 us
  Pallas kernels: 67.3 us -> 77.2 us
  starting transfers between devices: 14 us -> 20.6 us
  waiting for transfers between devices: 15.3 us -> 10.1 us
    unnamed x40 -> x15, local copies, waits for them, and re-layouts: 17.3 us -> 6.76 us
    pallas_call x1, Pallas kernels: 13.1 us -> 19.3 us  [local(): pl.pallas_call(functools.partial(edge_kernel, levels, lon), out_shape=[ed...]
    ppermute x3 -> x4, starting transfers between devices: 5.19 us -> 10.4 us  [both(): lax.ppermute(up, axis, [(i, (i + 1) % n) for i in range(ends)])]
    ppermute x3 -> x4, waiting for transfers between devices: 4.87 us -> 1.48 us  [both(): lax.ppermute(up, axis, [(i, (i + 1) % n) for i in range(ends)])]
    pallas_call x0 -> x1, Pallas kernels: none -> 2.83 us  [local(): pl.pallas_call(functools.partial(pack_kernel, tiles), out_shape=packed_sh...]
    ppermute x3 -> x4, waiting for transfers between devices: 10.4 us -> 8.64 us  [both(): lax.ppermute(down, axis, [((i + 1) % n, i) for i in range(ends)])]
    ppermute x3 -> x4, starting transfers between devices: 8.85 us -> 10.2 us  [both(): lax.ppermute(down, axis, [((i + 1) % n, i) for i in range(ends)])]
  transfers between devices with their start and end apart: 6 -> 8, of which waited for: 2 -> 3; matrix products, arithmetic and copies ran while one was open for 1% -> 2% of each run, Pallas kernels for 24% -> 26%
where the time goes in v4:
time: 118 us; the launch traced here: 117 us
  Pallas kernels  77.2 us (65%)
  starting transfers between devices  20.6 us (17%)
  waiting for transfers between devices  10.1 us (9%)
  local copies, waits for them, and re-layouts  6.78 us (6%)
  other arithmetic  1.89 us (2%)
    pallas_call x1, Pallas kernels, local(): pl.pallas_call(functools.partial(advect_kernel, lon, tiles), grid=(groups...  27.2 us
    pallas_call x1, Pallas kernels, local(): pl.pallas_call(functools.partial(inner_kernel, levels, lon, tiles), out_s...  21.5 us
    pallas_call x1, Pallas kernels, local(): pl.pallas_call(functools.partial(edge_kernel, levels, lon), out_shape=[ed...  19.3 us
    ppermute x4, starting transfers between devices, both(): lax.ppermute(up, axis, [(i, (i + 1) % n) for i in range(ends)])  10.4 us
    ppermute x4, starting transfers between devices, both(): lax.ppermute(down, axis, [((i + 1) % n, i) for i in range(ends)])  10.2 us
    ppermute x4, waiting for transfers between devices, both(): lax.ppermute(down, axis, [((i + 1) % n, i) for i in range(ends)])  8.64 us
    unnamed x15, local copies, waits for them, and re-layouts  6.76 us
    pallas_call x1, Pallas kernels, local(): pl.pallas_call(functools.partial(gather_kernel, levels, lon), out_shape=j...  6.42 us
  transfers between devices with their start and end apart: 8, of which 3 were waited for; matrix products, arithmetic and copies ran while one was open for 2% of the time, Pallas kernels for 26%

profile of v4, /device:TPU:0, one launch (start us, length us, event | category | flops | bytes accessed | tf_op | source)
XLA Modules:
  0.0 117.4 jit_solution(7256199205045520548)
XLA Ops:
  0.6 19.3 %physics_edge.1 = (f32[4,6,144,128]{3,2,1,0:T(8,128)}, f32[4,6,144,128]{3,2,1,0:T(8,128)}, f32[4,6,144,128]{3,2,1,0:T(8,128)}, f32[4,6,144,128]{3,2,1,0:T(8,128)}) custom-call(f32[13152,128]{1,0:T(8,128)} %bitcast.16, s32[16,128]{1,0:T(8,128)} %conv.3, s32[16,128]{1,0:T(8,128)} %micro.3, bf16[822,1024]{1,0:T(8,128)(2,1)} %bitcast.18, ...), custom_call_target="tpu_custom_call" | custom-call | flops 7168065536 | bytes 20467712 | tf_op jit(solution)/shard_map/physics_edge/pallas_call | solution.py:312
  19.9 0.4 collective-permute-start
  20.4 4.0 %collective-permute-start.1 = (f32[4,6,144,128]{3,2,1,0:T(8,128)}, f32[4,6,144,128]{3,2,1,0:T(8,128)}, u32[]{:S(2)}, u32[]{:S(2)}) collective-permute-start(f32[4,6,144,128]{3,2,1,0:T(8,128)} %get-tuple-element.15.lo), channel_id=1, source_target_pairs={{1,0},{2,1},{3,2},{4,3},{5,4},{6,5},{7,6},{0,7},{9,8},{10,9},{11,1... | collective-permute-start | bytes 5308424 | tf_op jit(solution)/shard_map/ppermute | solution.py:328
  24.4 0.0 copy-start
  24.4 1.5 %copy-done = f32[4,6,144,128]{3,2,1,0:T(8,128)S(1)} copy-done((f32[4,6,144,128]{3,2,1,0:T(8,128)S(1)}, f32[4,6,144,128]{3,2,1,0:T(8,128)}, u32[]{:S(2)}) %copy-start) | copy-done | bytes 1769496
  25.9 0.0 copy-start.1
  25.9 1.5 %copy-done.1 = f32[4,6,144,128]{3,2,1,0:T(8,128)S(1)} copy-done((f32[4,6,144,128]{3,2,1,0:T(8,128)S(1)}, f32[4,6,144,128]{3,2,1,0:T(8,128)}, u32[]{:S(2)}) %copy-start.1) | copy-done | bytes 1769496
  27.4 2.8 %pack_edges.1 = (f32[8,6,2,8,128]{4,3,2,1,0:T(8,128)S(1)}, f32[8,6,8,128]{3,2,1,0:T(8,128)}, f32[8,6,8,128]{3,2,1,0:T(8,128)}) custom-call(f32[4,6,144,128]{3,2,1,0:T(8,128)S(1)} %copy-done, f32[4,6,144,128]{3,2,1,0:T(8,128)S(1)} %copy-done.1), custom_call_target="tpu_custom_call" | custom-call | tf_op jit(solution)/shard_map/pack_edges/pallas_call | solution.py:336
  30.2 0.0 copy-start.5
  30.2 0.8 copy-done.5
  31.0 4.6 %collective-permute-start.2 = (f32[8,6,8,128]{3,2,1,0:T(8,128)}, f32[8,6,8,128]{3,2,1,0:T(8,128)}, u32[]{:S(2)}, u32[]{:S(2)}) collective-permute-start(f32[8,6,8,128]{3,2,1,0:T(8,128)} %get-tuple-element.19), channel_id=1, source_target_pairs={{0,8},{8,16},{16,24},{1,9},{9,17},{17,25},{2,10},{10,18},{18,26},{... | collective-permute-start | bytes 589832 | tf_op jit(solution)/shard_map/ppermute | solution.py:327
  35.5 1.3 %collective-permute-start.3 = (f32[8,6,8,128]{3,2,1,0:T(8,128)}, f32[8,6,8,128]{3,2,1,0:T(8,128)}, u32[]{:S(2)}, u32[]{:S(2)}) collective-permute-start(f32[8,6,8,128]{3,2,1,0:T(8,128)} %get-tuple-element.20), channel_id=1, source_target_pairs={{8,0},{16,8},{24,16},{9,1},{17,9},{25,17},{10,2},{18,10},{26,18},{... | collective-permute-start | bytes 589832 | tf_op jit(solution)/shard_map/ppermute | solution.py:328
  36.8 0.0 copy-start.4
  36.8 21.5 %physics_inner.1 = (f32[8,6,144,128]{3,2,1,0:T(8,128)}, f32[8,6,144,128]{3,2,1,0:T(8,128)}, f32[8,6,2,8,128]{4,3,2,1,0:T(8,128)}, f32[8,6,8,128]{3,2,1,0:T(8,128)}, f32[8,6,8,128]{3,2,1,0:T(8,128)}) custom-call(f32[13152,128]{1,0:T(8,128)} %bitcast.17, s32[16,128]{1,0:T(8,128)} %conv.3, s32[16,128]{1,0:T(8,128)} %micro.3, bf16[822,1024]{1,0:T(8,128)(2,1)} %bitcast.19, ...), custom_call_target="tpu_custom_call" | custom-call | flops 7168065536 | bytes 20467712 | tf_op jit(solution)/shard_map/physics_inner/pallas_call | solution.py:346
  58.3 0.0 copy-start.3
  58.3 5.4 %collective-permute-start.5 = (f32[8,6,8,128]{3,2,1,0:T(8,128)}, f32[8,6,8,128]{3,2,1,0:T(8,128)}, u32[]{:S(2)}, u32[]{:S(2)}) collective-permute-start(f32[8,6,8,128]{3,2,1,0:T(8,128)} %get-tuple-element.21), channel_id=1, source_target_pairs={{0,8},{8,16},{16,24},{1,9},{9,17},{17,25},{2,10},{10,18},{18,26},{... | collective-permute-start | bytes 589832 | tf_op jit(solution)/shard_map/ppermute | solution.py:327
  63.7 0.0 collective-permute-done.2
  63.7 1.3 %collective-permute-start.6 = (f32[8,6,8,128]{3,2,1,0:T(8,128)}, f32[8,6,8,128]{3,2,1,0:T(8,128)S(1)}, u32[]{:S(2)}, u32[]{:S(2)}) collective-permute-start(f32[8,6,8,128]{3,2,1,0:T(8,128)} %get-tuple-element.22), channel_id=1, source_target_pairs={{8,0},{16,8},{24,16},{9,1},{17,9},{25,17},{10,2},{18,10},{26,18},{... | collective-permute-start | bytes 589832 | tf_op jit(solution)/shard_map/ppermute | solution.py:328
  65.0 0.0 collective-permute-done.3
  65.0 1.5 %collective-permute-done.5 = f32[8,6,8,128]{3,2,1,0:T(8,128)} collective-permute-done((f32[8,6,8,128]{3,2,1,0:T(8,128)}, f32[8,6,8,128]{3,2,1,0:T(8,128)}, u32[]{:S(2)}, u32[]{:S(2)}) %collective-permute-start.5) | collective-permute-done | bytes 196640 | tf_op jit(solution)/shard_map/ppermute | solution.py:327
  66.5 5.5 %collective-permute-done.6 = f32[8,6,8,128]{3,2,1,0:T(8,128)S(1)} collective-permute-done((f32[8,6,8,128]{3,2,1,0:T(8,128)}, f32[8,6,8,128]{3,2,1,0:T(8,128)S(1)}, u32[]{:S(2)}, u32[]{:S(2)}) %collective-permute-start.6) | collective-permute-done | bytes 196640 | tf_op jit(solution)/shard_map/ppermute | solution.py:328
  72.0 1.2 select_bitcast_fusion.1
  73.2 0.1 collective-permute-start.4
  73.3 0.0 copy-done.4
  73.3 0.0 copy-done.3
  73.3 0.0 copy-start.2
  73.3 2.0 %copy-done.2 = f32[8,6,144,128]{3,2,1,0:T(8,128)S(1)} copy-done((f32[8,6,144,128]{3,2,1,0:T(8,128)S(1)}, f32[8,6,144,128]{3,2,1,0:T(8,128)}, u32[]{:S(2)}) %copy-start.2) | copy-done | bytes 3538968
  75.3 6.4 %gather_tendency.1 = f32[13152,128]{1,0:T(8,128)} custom-call(f32[4,6,144,128]{3,2,1,0:T(8,128)S(1)} %copy-done.3, f32[8,6,144,128]{3,2,1,0:T(8,128)S(1)} %copy-done.2, f32[4,6,144,128]{3,2,1,0:T(8,128)S(1)} %copy-done.4), custom_call_target="tpu_custom_call" | custom-call | flops 1683456 | bytes 13467648 | tf_op jit(solution)/shard_map/gather_tendency/pallas_call | solution.py:362
  81.8 0.6 add_select_fusion.inside
  82.4 0.0 collective-permute-done.4
  82.4 3.6 %collective-permute-start.7 = (f32[4,6,2,8,128]{4,3,2,1,0:T(8,128)S(1)}, f32[4,6,2,8,128]{4,3,2,1,0:T(8,128)S(1)}, u32[]{:S(2)}, u32[]{:S(2)}) collective-permute-start(f32[4,6,2,8,128]{4,3,2,1,0:T(8,128)S(1)} %get-tuple-element.27), channel_id=1, source_target_pairs={{1,0},{2,1},{3,2},{4,3},{5,4},{6,5},{7,6},{0,7},{9,8},{10,9},{11,1... | collective-permute-start | bytes 589832 | tf_op jit(solution)/shard_map/ppermute | solution.py:328
  86.0 3.1 %collective-permute-done.7 = f32[4,6,2,8,128]{4,3,2,1,0:T(8,128)S(1)} collective-permute-done((f32[4,6,2,8,128]{4,3,2,1,0:T(8,128)S(1)}, f32[4,6,2,8,128]{4,3,2,1,0:T(8,128)S(1)}, u32[]{:S(2)}, u32[]{:S(2)}) %collective-permute-start.7) | collective-permute-done | bytes 196640 | tf_op jit(solution)/shard_map/ppermute | solution.py:328
  89.2 0.0 copy-start.6
  89.2 0.0 collective-permute-done.left
  89.2 0.0 collective-permute-done.1.right
  89.2 1.0 copy-done.6
  90.2 27.2 %advect.1 = f32[6,2192,128]{2,1,0:T(8,128)} custom-call(f32[4,6,144,128]{3,2,1,0:T(8,128)} %collective-permute-done.left, f32[4,6,144,128]{3,2,1,0:T(8,128)} %get-tuple-element.15.lo, f32[8,6,144,128]{3,2,1,0:T(8,128)} %get-tuple-element.17.mid, f32[4,6,144,128]{3,2,1,0:T(8,128)} %get-tuple-element.14.hi, f32[4,6,144,128]{3,2,1,0:T(8,128)} %collective-permute-done.1.right, ...), custom_call_target="tpu_custom_call" | custom-call | flops 101007360 | bytes 20201472 | tf_op jit(solution)/shard_map/advect/pallas_call | solution.py:393
  (10 shorter events, 0.1 us)
Async XLA Ops:
  19.9 69.3 %collective-permute-start = (f32[4,6,144,128]{3,2,1,0:T(8,128)}, f32[4,6,144,128]{3,2,1,0:T(8,128)}, u32[]{:S(2)}, u32[]{:S(2)}) collective-permute-start(f32[4,6,144,128]{3,2,1,0:T(8,128)} %get-tuple-element.14.hi), channel_id=1, source_target_pairs={{0,1},{1,2},{2,3},{3,4},{4,5},{5,6},{6,7},{7,0},{8,9},{9,10},{10,1... | collective-permute-start | bytes 5308424 | tf_op jit(solution)/shard_map/ppermute | solution.py:327
  20.4 68.9 %collective-permute-start.1 = (f32[4,6,144,128]{3,2,1,0:T(8,128)}, f32[4,6,144,128]{3,2,1,0:T(8,128)}, u32[]{:S(2)}, u32[]{:S(2)}) collective-permute-start(f32[4,6,144,128]{3,2,1,0:T(8,128)} %get-tuple-element.15.lo), channel_id=1, source_target_pairs={{1,0},{2,1},{3,2},{4,3},{5,4},{6,5},{7,6},{0,7},{9,8},{10,9},{11,1... | collective-permute-start | bytes 5308424 | tf_op jit(solution)/shard_map/ppermute | solution.py:328
  24.4 1.5 %copy-start = (f32[4,6,144,128]{3,2,1,0:T(8,128)S(1)}, f32[4,6,144,128]{3,2,1,0:T(8,128)}, u32[]{:S(2)}) copy-start(f32[4,6,144,128]{3,2,1,0:T(8,128)} %get-tuple-element.15.lo) | copy-start | bytes 5308420
  25.9 1.5 %copy-start.1 = (f32[4,6,144,128]{3,2,1,0:T(8,128)S(1)}, f32[4,6,144,128]{3,2,1,0:T(8,128)}, u32[]{:S(2)}) copy-start(f32[4,6,144,128]{3,2,1,0:T(8,128)} %get-tuple-element.14.hi) | copy-start | bytes 5308420
  30.2 0.8 copy-start.5
  31.0 32.7 %collective-permute-start.2 = (f32[8,6,8,128]{3,2,1,0:T(8,128)}, f32[8,6,8,128]{3,2,1,0:T(8,128)}, u32[]{:S(2)}, u32[]{:S(2)}) collective-permute-start(f32[8,6,8,128]{3,2,1,0:T(8,128)} %get-tuple-element.19), channel_id=1, source_target_pairs={{0,8},{8,16},{16,24},{1,9},{9,17},{17,25},{2,10},{10,18},{18,26},{... | collective-permute-start | bytes 589832 | tf_op jit(solution)/shard_map/ppermute | solution.py:327
  35.5 29.5 %collective-permute-start.3 = (f32[8,6,8,128]{3,2,1,0:T(8,128)}, f32[8,6,8,128]{3,2,1,0:T(8,128)}, u32[]{:S(2)}, u32[]{:S(2)}) collective-permute-start(f32[8,6,8,128]{3,2,1,0:T(8,128)} %get-tuple-element.20), channel_id=1, source_target_pairs={{8,0},{16,8},{24,16},{9,1},{17,9},{25,17},{10,2},{18,10},{26,18},{... | collective-permute-start | bytes 589832 | tf_op jit(solution)/shard_map/ppermute | solution.py:328
  36.8 36.5 %copy-start.4 = (f32[4,6,144,128]{3,2,1,0:T(8,128)S(1)}, f32[4,6,144,128]{3,2,1,0:T(8,128)}, u32[]{:S(2)}) copy-start(f32[4,6,144,128]{3,2,1,0:T(8,128)} %get-tuple-element.25.thi) | copy-start | bytes 5308420
  58.3 15.0 %copy-start.3 = (f32[4,6,144,128]{3,2,1,0:T(8,128)S(1)}, f32[4,6,144,128]{3,2,1,0:T(8,128)}, u32[]{:S(2)}) copy-start(f32[4,6,144,128]{3,2,1,0:T(8,128)} %get-tuple-element.23.tlo) | copy-start | bytes 5308420
  58.3 8.2 %collective-permute-start.5 = (f32[8,6,8,128]{3,2,1,0:T(8,128)}, f32[8,6,8,128]{3,2,1,0:T(8,128)}, u32[]{:S(2)}, u32[]{:S(2)}) collective-permute-start(f32[8,6,8,128]{3,2,1,0:T(8,128)} %get-tuple-element.21), channel_id=1, source_target_pairs={{0,8},{8,16},{16,24},{1,9},{9,17},{17,25},{2,10},{10,18},{18,26},{... | collective-permute-start | bytes 589832 | tf_op jit(solution)/shard_map/ppermute | solution.py:327
  63.7 8.3 %collective-permute-start.6 = (f32[8,6,8,128]{3,2,1,0:T(8,128)}, f32[8,6,8,128]{3,2,1,0:T(8,128)S(1)}, u32[]{:S(2)}, u32[]{:S(2)}) collective-permute-start(f32[8,6,8,128]{3,2,1,0:T(8,128)} %get-tuple-element.22), channel_id=1, source_target_pairs={{8,0},{16,8},{24,16},{9,1},{17,9},{25,17},{10,2},{18,10},{26,18},{... | collective-permute-start | bytes 589832 | tf_op jit(solution)/shard_map/ppermute | solution.py:328
  73.2 9.1 %collective-permute-start.4 = (f32[4,6,2,8,128]{4,3,2,1,0:T(8,128)S(1)}, f32[4,6,2,8,128]{4,3,2,1,0:T(8,128)S(1)}, u32[]{:S(2)}, u32[]{:S(2)}) collective-permute-start(f32[4,6,2,8,128]{4,3,2,1,0:T(8,128)S(1)} %fusion), channel_id=1, source_target_pairs={{0,1},{1,2},{2,3},{3,4},{4,5},{5,6},{6,7},{7,0},{8,9},{9,10},{10,1... | collective-permute-start | bytes 589832 | tf_op jit(solution)/shard_map/ppermute | solution.py:327
  73.3 2.0 %copy-start.2 = (f32[8,6,144,128]{3,2,1,0:T(8,128)S(1)}, f32[8,6,144,128]{3,2,1,0:T(8,128)}, u32[]{:S(2)}) copy-start(f32[8,6,144,128]{3,2,1,0:T(8,128)} %get-tuple-element.24.tmid) | copy-start | bytes 10616836
  82.4 6.8 %collective-permute-start.7 = (f32[4,6,2,8,128]{4,3,2,1,0:T(8,128)S(1)}, f32[4,6,2,8,128]{4,3,2,1,0:T(8,128)S(1)}, u32[]{:S(2)}, u32[]{:S(2)}) collective-permute-start(f32[4,6,2,8,128]{4,3,2,1,0:T(8,128)S(1)} %get-tuple-element.27), channel_id=1, source_target_pairs={{1,0},{2,1},{3,2},{4,3},{5,4},{6,5},{7,6},{0,7},{9,8},{10,9},{11,1... | collective-permute-start | bytes 589832 | tf_op jit(solution)/shard_map/ppermute | solution.py:328
  89.2 1.0 copy-start.6

commit v5 on v3

--- a/solution.py
+++ b/solution.py
@@ -306,7 +306,7 @@
         in_specs=[full] * 6,
         out_specs=[full] * 4,
         scratch_shapes=scratch,
-        compiler_params=limit(32),
+        compiler_params=limit(56),
         cost_estimate=cost(2 * HALO),
         name="physics_edge",
     )(cells, conv_mask, micro_mask, w_in.T, w_hidden, w_out)
@@ -334,7 +334,7 @@
         in_specs=[full] * 8,
         out_specs=[full] * 5,
         scratch_shapes=scratch,
-        compiler_params=limit(36),
+        compiler_params=limit(56),
         cost_estimate=cost(lon - 2 * HALO),
         name="physics_inner",
     )(cells, conv_mask, micro_mask, w_in.T, w_hidden, w_out, lo, hi)

time: 117 us -> 112 us (0.957)
  local copies, waits for them, and re-layouts: 17.3 us -> 4.97 us
  Pallas kernels: 67.3 us -> 75.3 us
    unnamed x40 -> x22, local copies, waits for them, and re-layouts: 17.3 us -> 4.97 us
    pallas_call x1, Pallas kernels: 13.1 us -> 19.1 us  [local(): pl.pallas_call(functools.partial(edge_kernel, levels, lon), out_shape=[ed...]
    pallas_call x1, Pallas kernels: 21.7 us -> 24.8 us  [local(): pl.pallas_call(functools.partial(inner_kernel, levels, lon, tiles), out_s...]
  transfers between devices with their start and end apart: 6 -> 6, of which waited for: 2 -> 2; matrix products, arithmetic and copies ran while one was open for 1% -> 1% of each run, Pallas kernels for 24% -> 28%
where the time goes in v5:
time: 112 us
  Pallas kernels  75.3 us (67%)
  waiting for transfers between devices  15.2 us (14%)
  starting transfers between devices  14.1 us (13%)
  local copies, waits for them, and re-layouts  4.97 us (4%)
  other arithmetic  1.31 us (1%)
    pallas_call x1, Pallas kernels, local(): pl.pallas_call(functools.partial(advect_kernel, lon, tiles), grid=(groups...  25 us
    pallas_call x1, Pallas kernels, local(): pl.pallas_call(functools.partial(inner_kernel, levels, lon, tiles), out_s...  24.8 us
    pallas_call x1, Pallas kernels, local(): pl.pallas_call(functools.partial(edge_kernel, levels, lon), out_shape=[ed...  19.1 us
    ppermute x3, waiting for transfers between devices, both(): lax.ppermute(down, axis, [((i + 1) % n, i) for i in range(ends)])  10.4 us
    ppermute x3, starting transfers between devices, both(): lax.ppermute(down, axis, [((i + 1) % n, i) for i in range(ends)])  8.84 us
    pallas_call x1, Pallas kernels, local(): pl.pallas_call(functools.partial(gather_kernel, levels, lon), out_shape=j...  6.43 us
    ppermute x3, starting transfers between devices, both(): lax.ppermute(up, axis, [(i, (i + 1) % n) for i in range(ends)])  5.22 us
    unnamed x22, local copies, waits for them, and re-layouts  4.97 us
  transfers between devices with their start and end apart: 6, of which 2 were waited for; matrix products, arithmetic and copies ran while one was open for 1% of the time, Pallas kernels for 28%

profile of v5, /device:TPU:0, one launch (start us, length us, event | category | flops | bytes accessed | tf_op | source)
XLA Modules:
  0.0 111.7 jit_solution(13728983936606095063)
XLA Ops:
  0.6 19.1 %physics_edge.1 = (f32[4,6,144,128]{3,2,1,0:T(8,128)}, f32[4,6,144,128]{3,2,1,0:T(8,128)}, f32[4,6,144,128]{3,2,1,0:T(8,128)}, f32[4,6,144,128]{3,2,1,0:T(8,128)}) custom-call(f32[13152,128]{1,0:T(8,128)} %bitcast.12, s32[16,128]{1,0:T(8,128)} %conv.3, s32[16,128]{1,0:T(8,128)} %micro.3, bf16[822,1024]{1,0:T(8,128)(2,1)} %bitcast.14, ...), custom_call_target="tpu_custom_call" | custom-call | flops 7168065536 | bytes 20467712 | tf_op jit(solution)/shard_map/physics_edge/pallas_call | solution.py:303
  19.7 0.5 collective-permute-start
  20.2 4.0 %collective-permute-start.1 = (f32[4,6,144,128]{3,2,1,0:T(8,128)}, f32[4,6,144,128]{3,2,1,0:T(8,128)S(1)}, u32[]{:S(2)}, u32[]{:S(2)}) collective-permute-start(f32[4,6,144,128]{3,2,1,0:T(8,128)} %get-tuple-element.12.lo), channel_id=1, source_target_pairs={{1,0},{2,1},{3,2},{4,3},{5,4},{6,5},{7,6},{0,7},{9,8},{10,9},{11,1... | collective-permute-start | bytes 5308424 | tf_op jit(solution)/shard_map/ppermute | solution.py:319
  24.2 24.8 %physics_inner.1 = (f32[8,6,144,128]{3,2,1,0:T(8,128)}, f32[8,6,144,128]{3,2,1,0:T(8,128)}, f32[16,6,2,8,128]{4,3,2,1,0:T(8,128)}, f32[16,6,8,128]{3,2,1,0:T(8,128)}, f32[16,6,8,128]{3,2,1,0:T(8,128)}) custom-call(f32[13152,128]{1,0:T(8,128)} %bitcast.13, s32[16,128]{1,0:T(8,128)} %conv.3, s32[16,128]{1,0:T(8,128)} %micro.3, bf16[822,1024]{1,0:T(8,128)(2,1)} %bitcast.15, ...), custom_call_target="tpu_custom_call" | custom-call | flops 7168065536 | bytes 20467712 | tf_op jit(solution)/shard_map/physics_inner/pallas_call | solution.py:325
  49.0 4.7 %collective-permute-start.2 = (f32[16,6,8,128]{3,2,1,0:T(8,128)}, f32[16,6,8,128]{3,2,1,0:T(8,128)}, u32[]{:S(2)}, u32[]{:S(2)}) collective-permute-start(f32[16,6,8,128]{3,2,1,0:T(8,128)} %get-tuple-element.15), channel_id=1, source_target_pairs={{0,8},{8,16},{16,24},{1,9},{9,17},{17,25},{2,10},{10,18},{18,26},{... | collective-permute-start | bytes 1179656 | tf_op jit(solution)/shard_map/ppermute | solution.py:318
  53.7 1.3 %collective-permute-start.3 = (f32[16,6,8,128]{3,2,1,0:T(8,128)}, f32[16,6,8,128]{3,2,1,0:T(8,128)}, u32[]{:S(2)}, u32[]{:S(2)}) collective-permute-start(f32[16,6,8,128]{3,2,1,0:T(8,128)} %get-tuple-element.16), channel_id=1, source_target_pairs={{8,0},{16,8},{24,16},{9,1},{17,9},{25,17},{10,2},{18,10},{26,18},{... | collective-permute-start | bytes 1179656 | tf_op jit(solution)/shard_map/ppermute | solution.py:319
  55.0 0.0 copy-start.5
  55.0 4.8 %collective-permute-done.2 = f32[16,6,8,128]{3,2,1,0:T(8,128)} collective-permute-done((f32[16,6,8,128]{3,2,1,0:T(8,128)}, f32[16,6,8,128]{3,2,1,0:T(8,128)}, u32[]{:S(2)}, u32[]{:S(2)}) %collective-permute-start.2) | collective-permute-done | bytes 393248 | tf_op jit(solution)/shard_map/ppermute | solution.py:318
  59.9 10.4 %collective-permute-done.3 = f32[16,6,8,128]{3,2,1,0:T(8,128)} collective-permute-done((f32[16,6,8,128]{3,2,1,0:T(8,128)}, f32[16,6,8,128]{3,2,1,0:T(8,128)}, u32[]{:S(2)}, u32[]{:S(2)}) %collective-permute-start.3) | collective-permute-done | bytes 393248 | tf_op jit(solution)/shard_map/ppermute | solution.py:319
  70.2 1.2 %select_bitcast_fusion.1 = (f32[16,6,1,8,128]{4,3,2,1,0:T(8,128)S(1)}, f32[16,6,1,8,128]{4,3,2,1,0:T(8,128)S(1)}) fusion(f32[16,6,8,128]{3,2,1,0:T(8,128)} %collective-permute-done.2, f32[16,6,8,128]{3,2,1,0:T(8,128)} %collective-permute-done.3, pred[8,128]{1,0:T(8,128)(4,1)S(1)} %select_compare_fusion.1), kind=kLoop, calls=%fused_computation.2 | loop fusion | flops 196608 | bytes 1573888 | tf_op jit(solution)/shard_map/stack | solution.py:353
  71.4 0.1 collective-permute-start.4
  71.5 3.5 %collective-permute-start.5 = (f32[4,6,2,8,128]{4,3,2,1,0:T(8,128)S(1)}, f32[4,6,2,8,128]{4,3,2,1,0:T(8,128)S(1)}, u32[]{:S(2)}, u32[]{:S(2)}) collective-permute-start(f32[4,6,2,8,128]{4,3,2,1,0:T(8,128)S(1)} %get-tuple-element.23), channel_id=1, source_target_pairs={{1,0},{2,1},{3,2},{4,3},{5,4},{6,5},{7,6},{0,7},{9,8},{10,9},{11,1... | collective-permute-start | bytes 589832 | tf_op jit(solution)/shard_map/ppermute | solution.py:319
  75.1 0.0 copy-done.5
  75.1 0.0 copy-start
  75.1 2.0 %copy-done = f32[8,6,144,128]{3,2,1,0:T(8,128)S(1)} copy-done((f32[8,6,144,128]{3,2,1,0:T(8,128)S(1)}, f32[8,6,144,128]{3,2,1,0:T(8,128)}, u32[]{:S(2)}) %copy-start) | copy-done | bytes 3538968
  77.1 0.0 copy-start.6
  77.1 1.5 %copy-done.6 = f32[4,6,144,128]{3,2,1,0:T(8,128)S(1)} copy-done((f32[4,6,144,128]{3,2,1,0:T(8,128)S(1)}, f32[4,6,144,128]{3,2,1,0:T(8,128)}, u32[]{:S(2)}) %copy-start.6) | copy-done | bytes 1769496
  78.5 0.0 copy-start.1
  78.5 0.0 copy-start.3
  78.5 0.0 copy-start.4
  78.5 0.0 copy-start.7
  78.5 0.0 copy-start.8
  78.6 0.0 copy-start.9
  78.6 0.0 copy-start.10
  78.6 6.4 %gather_tendency.1 = f32[13152,128]{1,0:T(8,128)} custom-call(f32[4,6,144,128]{3,2,1,0:T(8,128)S(1)} %copy-done.5, f32[8,6,144,128]{3,2,1,0:T(8,128)S(1)} %copy-done, f32[4,6,144,128]{3,2,1,0:T(8,128)S(1)} %copy-done.6), custom_call_target="tpu_custom_call" | custom-call | flops 1683456 | bytes 13467648 | tf_op jit(solution)/shard_map/gather_tendency/pallas_call | solution.py:343
  85.0 0.0 copy-start.2
  85.0 0.0 collective-permute-done.4
  85.0 0.0 collective-permute-done.5
  85.0 0.1 pad_maximum_fusion.halo
  85.1 0.0 collective-permute-done.left
  85.1 0.0 collective-permute-done.1.right
  85.1 0.0 copy-done.1
  85.2 0.0 copy-done.3
  85.2 0.0 copy-done.4
  85.2 0.0 copy-done.7
  85.2 0.0 copy-done.8
  85.2 0.0 copy-done.9
  85.2 0.0 copy-done.10
  85.2 1.5 %copy-done.2 = bf16[2,9,256,256]{3,2,1,0:T(8,128)(2,1)S(1)} copy-done((bf16[2,9,256,256]{3,2,1,0:T(8,128)(2,1)S(1)}, bf16[2,9,256,256]{3,2,1,0:T(8,128)(2,1)}, u32[]{:S(2)}) %copy-start.2) | copy-done | bytes 2359320
  86.7 25.0 %advect.1 = f32[6,2192,128]{2,1,0:T(8,128)} custom-call(f32[4,6,144,128]{3,2,1,0:T(8,128)S(1)} %collective-permute-done.left, f32[4,6,144,128]{3,2,1,0:T(8,128)S(1)} %copy-done.3, f32[8,6,144,128]{3,2,1,0:T(8,128)S(1)} %copy-done.1, f32[4,6,144,128]{3,2,1,0:T(8,128)S(1)} %copy-done.4, f32[4,6,144,128]{3,2,1,0:T(8,128)S(1)} %collective-permute-done.1.right, ...), custom_call_target="tpu_custom_call" | custom-call | flops 101007360 | bytes 20201472 | tf_op jit(solution)/shard_map/advect/pallas_call | solution.py:370
  (6 shorter events, 0.1 us)
Async XLA Ops:
  19.7 65.4 %collective-permute-start = (f32[4,6,144,128]{3,2,1,0:T(8,128)}, f32[4,6,144,128]{3,2,1,0:T(8,128)S(1)}, u32[]{:S(2)}, u32[]{:S(2)}) collective-permute-start(f32[4,6,144,128]{3,2,1,0:T(8,128)} %get-tuple-element.11.hi), channel_id=1, source_target_pairs={{0,1},{1,2},{2,3},{3,4},{4,5},{5,6},{6,7},{7,0},{8,9},{9,10},{10,1... | collective-permute-start | bytes 5308424 | tf_op jit(solution)/shard_map/ppermute | solution.py:318
  20.2 65.0 %collective-permute-start.1 = (f32[4,6,144,128]{3,2,1,0:T(8,128)}, f32[4,6,144,128]{3,2,1,0:T(8,128)S(1)}, u32[]{:S(2)}, u32[]{:S(2)}) collective-permute-start(f32[4,6,144,128]{3,2,1,0:T(8,128)} %get-tuple-element.12.lo), channel_id=1, source_target_pairs={{1,0},{2,1},{3,2},{4,3},{5,4},{6,5},{7,6},{0,7},{9,8},{10,9},{11,1... | collective-permute-start | bytes 5308424 | tf_op jit(solution)/shard_map/ppermute | solution.py:319
  49.0 10.9 %collective-permute-start.2 = (f32[16,6,8,128]{3,2,1,0:T(8,128)}, f32[16,6,8,128]{3,2,1,0:T(8,128)}, u32[]{:S(2)}, u32[]{:S(2)}) collective-permute-start(f32[16,6,8,128]{3,2,1,0:T(8,128)} %get-tuple-element.15), channel_id=1, source_target_pairs={{0,8},{8,16},{16,24},{1,9},{9,17},{17,25},{2,10},{10,18},{18,26},{... | collective-permute-start | bytes 1179656 | tf_op jit(solution)/shard_map/ppermute | solution.py:318
  53.7 16.6 %collective-permute-start.3 = (f32[16,6,8,128]{3,2,1,0:T(8,128)}, f32[16,6,8,128]{3,2,1,0:T(8,128)}, u32[]{:S(2)}, u32[]{:S(2)}) collective-permute-start(f32[16,6,8,128]{3,2,1,0:T(8,128)} %get-tuple-element.16), channel_id=1, source_target_pairs={{8,0},{16,8},{24,16},{9,1},{17,9},{25,17},{10,2},{18,10},{26,18},{... | collective-permute-start | bytes 1179656 | tf_op jit(solution)/shard_map/ppermute | solution.py:319
  55.0 20.1 %copy-start.5 = (f32[4,6,144,128]{3,2,1,0:T(8,128)S(1)}, f32[4,6,144,128]{3,2,1,0:T(8,128)}, u32[]{:S(2)}) copy-start(f32[4,6,144,128]{3,2,1,0:T(8,128)} %get-tuple-element.17.tlo) | copy-start | bytes 5308420
  71.4 13.6 %collective-permute-start.4 = (f32[4,6,2,8,128]{4,3,2,1,0:T(8,128)S(1)}, f32[4,6,2,8,128]{4,3,2,1,0:T(8,128)S(1)}, u32[]{:S(2)}, u32[]{:S(2)}) collective-permute-start(f32[4,6,2,8,128]{4,3,2,1,0:T(8,128)S(1)} %get-tuple-element.22), channel_id=1, source_target_pairs={{0,1},{1,2},{2,3},{3,4},{4,5},{5,6},{6,7},{7,0},{8,9},{9,10},{10,1... | collective-permute-start | bytes 589832 | tf_op jit(solution)/shard_map/ppermute | solution.py:318
  71.5 13.5 %collective-permute-start.5 = (f32[4,6,2,8,128]{4,3,2,1,0:T(8,128)S(1)}, f32[4,6,2,8,128]{4,3,2,1,0:T(8,128)S(1)}, u32[]{:S(2)}, u32[]{:S(2)}) collective-permute-start(f32[4,6,2,8,128]{4,3,2,1,0:T(8,128)S(1)} %get-tuple-element.23), channel_id=1, source_target_pairs={{1,0},{2,1},{3,2},{4,3},{5,4},{6,5},{7,6},{0,7},{9,8},{10,9},{11,1... | collective-permute-start | bytes 589832 | tf_op jit(solution)/shard_map/ppermute | solution.py:319
  75.1 2.0 %copy-start = (f32[8,6,144,128]{3,2,1,0:T(8,128)S(1)}, f32[8,6,144,128]{3,2,1,0:T(8,128)}, u32[]{:S(2)}) copy-start(f32[8,6,144,128]{3,2,1,0:T(8,128)} %get-tuple-element.18.tmid) | copy-start | bytes 10616836
  77.1 1.5 %copy-start.6 = (f32[4,6,144,128]{3,2,1,0:T(8,128)S(1)}, f32[4,6,144,128]{3,2,1,0:T(8,128)}, u32[]{:S(2)}) copy-start(f32[4,6,144,128]{3,2,1,0:T(8,128)} %get-tuple-element.19.thi) | copy-start | bytes 5308420
  78.5 6.6 %copy-start.1 = (f32[8,6,144,128]{3,2,1,0:T(8,128)S(1)}, f32[8,6,144,128]{3,2,1,0:T(8,128)}, u32[]{:S(2)}) copy-start(f32[8,6,144,128]{3,2,1,0:T(8,128)} %get-tuple-element.13.mid) | copy-start | bytes 10616836
  78.5 6.6 %copy-start.3 = (f32[4,6,144,128]{3,2,1,0:T(8,128)S(1)}, f32[4,6,144,128]{3,2,1,0:T(8,128)}, u32[]{:S(2)}) copy-start(f32[4,6,144,128]{3,2,1,0:T(8,128)} %get-tuple-element.12.lo) | copy-start | bytes 5308420
  78.5 6.6 %copy-start.4 = (f32[4,6,144,128]{3,2,1,0:T(8,128)S(1)}, f32[4,6,144,128]{3,2,1,0:T(8,128)}, u32[]{:S(2)}) copy-start(f32[4,6,144,128]{3,2,1,0:T(8,128)} %get-tuple-element.11.hi) | copy-start | bytes 5308420
  78.5 6.6 %copy-start.7 = (f32[16,6,2,8,128]{4,3,2,1,0:T(8,128)S(1)}, f32[16,6,2,8,128]{4,3,2,1,0:T(8,128)}, u32[]{:S(2)}) copy-start(f32[16,6,2,8,128]{4,3,2,1,0:T(8,128)} %get-tuple-element.14.px) | copy-start | bytes 2359300
  78.5 6.6 %copy-start.8 = (bf16[2,256,256]{2,1,0:T(8,128)(2,1)S(1)}, bf16[2,256,256]{2,1,0:T(8,128)(2,1)}, u32[]{:S(2)}) copy-start(bf16[2,256,256]{2,1,0:T(8,128)(2,1)} %constant.41.clone.m_own) | copy-start | bytes 786436
  78.6 6.6 %copy-start.9 = (bf16[2,256,256]{2,1,0:T(8,128)(2,1)S(1)}, bf16[2,256,256]{2,1,0:T(8,128)(2,1)}, u32[]{:S(2)}) copy-start(bf16[2,256,256]{2,1,0:T(8,128)(2,1)} %constant.40.clone.m_packed) | copy-start | bytes 786436
  78.6 6.6 %copy-start.10 = (bf16[256,256]{1,0:T(8,128)(2,1)S(1)}, bf16[256,256]{1,0:T(8,128)(2,1)}, u32[]{:S(2)}) copy-start(bf16[256,256]{1,0:T(8,128)(2,1)} %constant.38.clone.m_center) | copy-start | bytes 393220
  85.0 1.7 %copy-start.2 = (bf16[2,9,256,256]{3,2,1,0:T(8,128)(2,1)S(1)}, bf16[2,9,256,256]{3,2,1,0:T(8,128)(2,1)}, u32[]{:S(2)}) copy-start(bf16[2,9,256,256]{3,2,1,0:T(8,128)(2,1)} %constant.39.clone.m_edges) | copy-start | bytes 7077892
